TPU v7x, 128 devices: a whole 4x4x4 slice. The times are simulated.
128 devices in a mesh: lat: 16 (over z, y_hi, core), lon: 8 (over y_lo, x).
Axes of the slice: x: 4, y: 4 (y_hi: 2, y_lo: 2; y = y_hi * 2 + y_lo), z: 4, core: 2. Of those that a mesh axis runs over, the one named last changes fastest.
Arguments:
- fields: float32 [6, 32, 256, 2880], P(None, None, 'lat', 'lon'), may hold values from -6 to 6
- inv_cos: float32 [256], P('lat'), may hold values from 0.9 to 8.8
- coupling_lon: float32 [6, 6], replicated, may hold values from -0.4 to 0.4
- coupling_lat: float32 [6, 6], replicated, may hold values from -1.5 to 1.5
- polar_rows: int32 [56], replicated, may hold values from 0 to 255, as said below
- bands: int32 [56], replicated, may hold values from 32 to 1024, as said below
Outputs:
- smoothed_fields: float32 [6, 32, 256, 2880], P(None, None, 'lat', 'lon')
Inputs may be any that keep to these rules, and one draw needn't show every extreme that they name: `polar_rows`: ascending and distinct; each of the first 2 and the last 2 blocks of 16 rows holds exactly 14 of them, rows 0 and 255 are always listed, and no other row is listed. `bands`: the band width of the row at the same position of polar_rows: with d the row's distance from its nearest end row (0 or 255) and e the largest such distance among the listed rows at that end, it is 32 + ((992) d) // e.
All inputs are finite; a program needn't handle non-finite values.
Results may differ from a plain program's by a relative error of at most 0.00005.
Values sent between devices are 32-bit elements; how exact they have to be, the bound alone decides.
A program may use at most 128 MiB of HBM per device.

v0:
```python
import math

import jax
import jax.numpy as jnp
from jax import lax
from jax.sharding import PartitionSpec as P

KMAX = 1024
CAP = 14


def padded_2(cells, sides, width, closed):
    for axis, dim in sides:
        count = lax.axis_size(axis)
        ends = count if closed else count - 1
        head = lax.slice_in_dim(cells, 0, width, axis=dim)
        tail = lax.slice_in_dim(cells, cells.shape[dim] - width, cells.shape[dim], axis=dim)
        cells = jnp.concatenate(
            [
                lax.ppermute(tail, axis, [(i, (i + 1) % count) for i in range(ends)]),
                cells,
                lax.ppermute(head, axis, [((i + 1) % count, i) for i in range(ends)]),
            ],
            axis=dim,
        )
    return cells


def difference(padded, axis, count):

    def shifted(offset):
        return lax.slice_in_dim(padded, 3 + offset, 3 + offset + count, axis=axis)

    return (
        45.0 * (shifted(1) - shifted(-1))
        - 9.0 * (shifted(2) - shifted(-2))
        + (shifted(3) - shifted(-3))
    ) / 60.0


def fourier_table(length, modes):
    cells = jnp.arange(length, dtype=jnp.int32)
    waves = jnp.arange(modes, dtype=jnp.int32)
    phase = (cells[:, None] * waves[None, :] % length).astype(jnp.float32) * (
        2.0 * math.pi / length
    )
    return jnp.concatenate([jnp.cos(phase), jnp.sin(phase)], axis=1)


def mode_weights(band_each, modes, length):
    columns = jnp.arange(2 * modes, dtype=jnp.int32) % modes
    keep = columns[None, :] < band_each[:, None]
    factor = jnp.where(columns == 0, 1.0, 2.0) / length
    return jnp.where(keep, factor[None, :], 0.0).astype(jnp.float32)


def slot_table(polar_rows, bands, tile, rows_dev, slot_count):
    owner_tile = polar_rows // rows_dev
    local_row = polar_rows % rows_dev
    order = jnp.arange(polar_rows.shape[0], dtype=jnp.int32)
    earlier = (owner_tile[:, None] == owner_tile[None, :]) & (order[None, :] < order[:, None])
    slot_rank = jnp.sum(earlier.astype(jnp.int32), axis=1)
    mine = (owner_tile == tile).astype(jnp.int32)
    slot_ids = jnp.arange(slot_count, dtype=jnp.int32)
    in_slot = mine[None, :] * (slot_rank[None, :] == slot_ids[:, None]).astype(jnp.int32)
    row_ids = jnp.arange(rows_dev, dtype=jnp.int32)
    chosen = (local_row[:, None] == row_ids[None, :]).astype(jnp.int32)
    selection = jnp.sum(in_slot[:, :, None] * chosen[None, :, :], axis=1)
    band_slot = jnp.sum(in_slot * bands[None, :], axis=1)
    return (selection, band_slot)


def polar_filter(block, band_slot):
    field_count, level_count, slot_count, width = block.shape
    item_rows = block.reshape(field_count * level_count * slot_count, width)
    gathered = lax.all_to_all(item_rows, "lon", split_axis=0, concat_axis=1, tiled=True)
    per_device = gathered.shape[0]
    length = gathered.shape[1]
    item_index = lax.axis_index("lon") * per_device + jnp.arange(per_device, dtype=jnp.int32)
    slot_of = item_index % slot_count
    slot_ids = jnp.arange(slot_count, dtype=jnp.int32)
    band_item = jnp.sum(
        jnp.where(slot_of[:, None] == slot_ids[None, :], band_slot[None, :], 0), axis=1
    )
    table = fourier_table(length, KMAX)
    spectra = jnp.dot(
        gathered, table, precision=lax.Precision.HIGHEST, preferred_element_type=jnp.float32
    )
    weighted = spectra * mode_weights(band_item, KMAX, length)
    smoothed = jnp.einsum("ik,nk->in", weighted, table, precision=lax.Precision.HIGHEST)
    returned = lax.all_to_all(smoothed, "lon", split_axis=1, concat_axis=0, tiled=True)
    return returned.reshape(field_count, level_count, slot_count, width)


def local(fields, inv_cos, coupling_lon, coupling_lat, polar_rows, bands):
    rows_dev = fields.shape[2]
    padded_lat = padded_2(fields, (("lat", 2),), 3, False)
    padded_lon = padded_2(fields, (("lon", 3),), 3, True)
    along_lat = difference(padded_lat, 2, rows_dev)
    along_lon = difference(padded_lon, 3, fields.shape[3]) * inv_cos[None, None, :, None]
    change = jnp.einsum("fg,glrn->flrn", coupling_lon, along_lon, precision=lax.Precision.HIGHEST)
    change = change + jnp.einsum(
        "fg,glrn->flrn", coupling_lat, along_lat, precision=lax.Precision.HIGHEST
    )
    predicted = fields + change
    my_tile = lax.axis_index("lat")
    selection, band_own = slot_table(polar_rows, bands, my_tile, rows_dev, CAP)
    select_float = selection.astype(jnp.float32)
    picked = jnp.einsum("cj,flje->flce", select_float, predicted, precision=lax.Precision.HIGHEST)
    result = polar_filter(picked, band_own)
    placed = jnp.einsum("cj,flce->flje", select_float, result, precision=lax.Precision.HIGHEST)
    row_taken = jnp.sum(selection, axis=0) > 0
    return jnp.where(row_taken[None, None, :, None], placed, predicted)


def solution(mesh):
    return jax.shard_map(
        local,
        mesh=mesh,
        in_specs=(P(None, None, "lat", "lon"), P("lat"), P(), P(), P(), P()),
        out_specs=P(None, None, "lat", "lon"),
        check_vma=False,
    )
```

profile of v0, /device:TPU:6, one launch (start us, length us, event | category | flops | bytes accessed | tf_op | source)
XLA Modules:
  0.0 343.3 jit_solution(7151937435482951808)
XLA Ops:
  0.0 0.0 copy-start
  0.0 0.0 copy-start.2
  0.0 2.9 fusion.62
  3.0 1.0 copy.66
  4.0 2.7 collective-permute-start.3
  6.7 1.0 copy.65
  7.7 0.0 copy-start.7
  7.7 1.4 collective-permute-start.2
  9.1 0.0 copy-done.2
  9.1 0.5 fusion.61
  9.7 0.8 copy.64
  10.5 1.5 collective-permute-start.1
  12.0 0.8 copy.63
  12.8 0.6 collective-permute-start
  13.4 0.0 copy-done.7
  13.4 0.0 copy-done.6
  13.4 0.2 convert_reduce_fusion
  13.6 0.0 copy-done.5
  13.6 0.1 multiply_reduce_fusion.2
  13.8 0.3 multiply_reduce_fusion.1
  14.1 6.7 %collective-permute-done = f32[6,32,16,3]{1,2,3,0:T(8,128)S(1)} collective-permute-done((f32[6,32,16,3]{1,2,3,0:T(8,128)S(1)}, f32[6,32,16,3]{1,2,3,0:T(8,128)S(1)}, u32[]{:S(2)}, u32[]{:S(2)}) %collective-permute-start) | collective-permute-done | bytes 36896 | tf_op jit(solution)/shard_map/ppermute | solution.py:22
  20.8 0.8 copy.42
  21.5 0.0 collective-permute-done.1
  21.5 0.0 slice-start
  21.6 1.9 copy.44
  23.5 26.3 %fusion.18 = (f32[6,32,16,360]{3,2,1,0:T(8,128)}, f32[6,32,19,360]{3,2,1,0:T(8,128)}) fusion(f32[6,32,16,3]{3,2,1,0:T(8,128)} %copy.44, f32[6,32,16,3]{3,2,1,0:T(8,128)S(1)} %copy.42, f32[6,32,16,360]{3,2,1,0:T(8,128)} %param.6, f32[16]{0:T(128)S(1)} %broadcast_multiply_fusion), kind=kLoop, calls=%fused_computation.31 | loop fusion | flops 15482879 | bytes 13934656 | tf_op jit(solution)/shard_map/mul | solution.py:100
  49.7 0.0 collective-permute-done.3
  49.8 1.8 copy.49
  51.5 0.0 collective-permute-done.2
  51.5 2.9 copy_dynamic-update-slice_fusion
  54.4 0.0 slice-done
  54.4 0.0 slice-done.1
  54.5 12.2 %fusion.29 = f32[6,32,16,360]{3,2,1,0:T(8,128)} fusion(f32[6,32,16,360]{3,2,1,0:T(8,128)S(1)} %bitcast.30, f32[6,32,3,360]{3,2,1,0:T(4,128)S(1)} %copy.49, f32[6,32,19,360]{3,2,1,0:T(8,128)} %copy_dynamic-update-slice_fusion), kind=kLoop, calls=%fused_computation.42 | loop fusion | flops 12165120 | bytes 22947840 | tf_op jit(solution)/shard_map/div | solution.py:34
  66.7 0.0 copy-done
  66.7 10.8 %fusion.9 = f32[32,16,360,6]{2,3,1,0:T(8,128)S(1)} fusion(f32[6,32,16,360]{3,2,1,0:T(8,128)} %fusion.29, f32[6,6]{1,0:T(8,128)S(1)} %copy-done), kind=kOutput, calls=%fused_computation.18 | convolution fusion | flops 79626240 | bytes 8847504 | tf_op jit(solution)/shard_map/fg,glrn->flrn/dot_general | solution.py:102
  77.5 0.0 copy-done.4
  77.5 14.3 %bitcast_add_fusion = f32[6,32,16,360]{3,0,2,1:T(8,128)S(1)} fusion(f32[6,32,16,360]{3,2,1,0:T(8,128)S(1)} %bitcast.30, f32[32,16,360,6]{2,3,1,0:T(8,128)S(1)} %fusion.9, f32[6,32,16,360]{3,2,1,0:T(8,128)} %get-tuple-element.9, f32[6,6]{1,0:T(8,128)S(1)} %copy-done.4), kind=kOutput, calls=%fused_computation.17 | convolution fusion | flops 81838080 | bytes 17694864 | tf_op jit(solution)/shard_map/fg,glrn->flrn/dot_general | solution.py:101
  91.8 0.0 copy-start.3
  91.8 2.7 copy-done.3
  94.5 6.0 %fusion.40 = f32[6,32,14,360]{3,2,1,0:T(8,128)} fusion(f32[6,32,16,360]{3,0,2,1:T(8,128)S(1)} %bitcast_add_fusion, s32[14,16]{1,0:T(8,128)S(1)} %get-tuple-element.6), kind=kOutput, calls=%fused_computation.54 | convolution fusion | flops 185794784 | bytes 8295296 | tf_op jit(solution)/shard_map/cj,flje->flce/dot_general | solution.py:109
  100.4 4.9 %all_to_all.26 = f32[8,336,360]{2,1,0:T(8,128)} reshape(f32[6,32,14,360]{3,2,1,0:T(8,128)} %fusion.40) | data formatting | bytes 7741440 | tf_op jit(solution)/shard_map/all_to_all | solution.py:76
  105.4 4.8 %all-to-all-start = ((f32[8,336,360]{2,1,0:T(8,128)}), f32[8,336,360]{2,1,0:T(8,128)}, u32[]{:S(2)}, u32[]{:S(2)}) async-start(f32[8,336,360]{2,1,0:T(8,128)} %all_to_all.26), calls=%async_computation | async-start | bytes 8257536 | tf_op jit(solution)/shard_map/all_to_all | solution.py:76
  110.2 0.1 select_reduce_fusion
  110.3 50.4 %fusion.6 = (f32[2880,1024]{1,0:T(8,128)}, f32[2880,1024]{1,0:T(8,128)}) fusion(), kind=kLoop, calls=%fused_computation.9 | loop fusion | flops 26542080 | bytes 23592960 | tf_op jit(solution)/shard_map/sin | solution.py:47
  160.6 12.2 %all-to-all-done = f32[8,336,360]{2,1,0:T(8,128)} async-done(((f32[8,336,360]{2,1,0:T(8,128)}), f32[8,336,360]{2,1,0:T(8,128)}, u32[]{:S(2)}, u32[]{:S(2)}) %all-to-all-start) | async-done | bytes 3870752 | tf_op jit(solution)/shard_map/all_to_all | solution.py:76
  172.8 5.5 %copy.53 = f32[336,8,360]{2,1,0:T(8,128)} copy(f32[336,8,360]{2,0,1:T(8,128)} %bitcast.8) | data formatting | bytes 7741440 | tf_op jit(solution)/shard_map/all_to_all | solution.py:76
  178.3 5.3 %all_to_all.29 = f32[336,2880]{1,0:T(8,128)} reshape(f32[336,8,360]{2,1,0:T(8,128)} %copy.53) | data formatting | bytes 7741440 | tf_op jit(solution)/shard_map/all_to_all | solution.py:76
  183.6 33.3 %fusion.37 = f32[336,2048]{1,0:T(8,128)S(1)} fusion(f32[336,2880]{1,0:T(8,128)} %all_to_all.29, f32[2880,1024]{1,0:T(8,128)} %get-tuple-element.17, f32[2880,1024]{1,0:T(8,128)} %get-tuple-element.18, f32[2048]{0:T(1024)S(1)} %select_multiply_fusion, s32[2048]{0:T(1024)S(1)} %add_select_fusion.1, s32[336]{0:T(512)S(1)} %select_reduce_fusion), kind=kOutput, calls=%fused_computation.53 | convolution fusion | flops 23789666304 | bytes 30233920 | tf_op jit(solution)/shard_map/dot_general | solution.py:86
  216.9 0.0 slice-done.4
  216.9 0.0 slice-done.5
  216.9 0.0 slice-done.6
  216.9 31.8 %fusion = f32[336,2880]{1,0:T(8,128)} fusion(f32[336,2048]{1,0:T(8,128)S(1)} %fusion.37, f32[2880,1024]{1,0:T(8,128)S(1)} %bitcast.34, f32[2880,1024]{1,0:T(8,128)} %get-tuple-element.18), kind=kOutput, calls=%fused_computation.1 | convolution fusion | flops 23787601920 | bytes 30216192 | tf_op jit(solution)/shard_map/ik,nk->in/dot_general | solution.py:90
  248.8 5.7 %all_to_all.30 = f32[336,8,360]{2,1,0:T(8,128)} reshape(f32[336,2880]{1,0:T(8,128)} %fusion) | data formatting | bytes 7741440 | tf_op jit(solution)/shard_map/all_to_all | solution.py:91
  254.5 4.9 %copy.54 = f32[336,8,360]{2,0,1:T(8,128)} copy(f32[336,8,360]{2,1,0:T(8,128)} %all_to_all.30) | data formatting | bytes 7741440 | tf_op jit(solution)/shard_map/all_to_all | solution.py:91
  259.4 5.8 %all-to-all-start.1 = ((f32[336,8,360]{2,0,1:T(8,128)}), f32[336,8,360]{2,0,1:T(8,128)}, u32[]{:S(2)}, u32[]{:S(2)}) async-start(f32[336,8,360]{2,0,1:T(8,128)} %copy.54), calls=%async_computation.1 | async-start | bytes 8257536 | tf_op jit(solution)/shard_map/all_to_all | solution.py:91
  265.1 60.3 %all-to-all-done.1 = f32[336,8,360]{2,0,1:T(8,128)} async-done(((f32[336,8,360]{2,0,1:T(8,128)}), f32[336,8,360]{2,0,1:T(8,128)}, u32[]{:S(2)}, u32[]{:S(2)}) %all-to-all-start.1) | async-done | bytes 3870752 | tf_op jit(solution)/shard_map/all_to_all | solution.py:91
  325.4 5.1 %reshape.94 = f32[6,32,14,360]{3,2,1,0:T(8,128)} reshape(f32[8,336,360]{2,1,0:T(8,128)} %bitcast.9) | data formatting | bytes 7741440 | tf_op jit(solution)/shard_map/reshape | solution.py:92
  330.5 6.1 %fusion.44 = f32[6,32,360,16]{2,3,1,0:T(8,128)S(1)} fusion(f32[6,32,14,360]{3,2,1,0:T(8,128)} %reshape.94, s32[14,16]{1,0:T(8,128)S(1)} %get-tuple-element.6), kind=kOutput, calls=%fused_computation.64 | convolution fusion | flops 185794784 | bytes 8295296 | tf_op jit(solution)/shard_map/cj,flce->flje/dot_general | solution.py:111
  336.6 0.0 slice-done.2
  336.6 0.0 slice-done.3
  336.6 0.0 copy-start.1
  336.6 3.1 bitcast_select_fusion
  339.7 3.0 copy.57
  342.8 0.0 copy-done.1
  (20 shorter events, 0.1 us)
Async XLA Ops:
  0.0 66.7 %copy-start = (f32[6,6]{1,0:T(8,128)S(1)}, f32[6,6]{1,0:T(8,128)}, u32[]{:S(2)}) copy-start(f32[6,6]{1,0:T(8,128)} %param.9) | copy-start | bytes 436
  0.0 9.1 %copy-start.2 = (f32[6,32,16,360]{3,2,1,0:T(8,128)S(1)}, f32[6,32,16,360]{3,2,1,0:T(8,128)}, u32[]{:S(2)}) copy-start(f32[6,32,16,360]{3,2,1,0:T(8,128)} %param.6) | copy-start | bytes 13271044
  4.0 45.8 %collective-permute-start.3 = (f32[6,32,3,360]{3,1,2,0:T(8,128)}, f32[6,32,3,360]{3,1,2,0:T(8,128)}, u32[]{:S(2)}, u32[]{:S(2)}) collective-permute-start(f32[6,32,3,360]{3,1,2,0:T(8,128)} %copy.66), channel_id=1, source_target_pairs={{0,8},{8,16},{16,24},{24,32},{32,40},{40,48},{48,56},{56,64},{64,7... | collective-permute-start | bytes 2488328 | tf_op jit(solution)/shard_map/ppermute | solution.py:20
  7.7 5.7 %copy-start.7 = (f32[16]{0:T(128)S(1)}, f32[16]{0:T(128)}, u32[]{:S(2)}) copy-start(f32[16]{0:T(128)} %param.7) | copy-start | bytes 196
  7.7 5.7 %copy-start.6 = (s32[56]{0:T(128)S(1)}, s32[56]{0:T(128)}, u32[]{:S(2)}) copy-start(s32[56]{0:T(128)} %param.10) | copy-start | bytes 676
  7.7 5.9 %copy-start.5 = (s32[56]{0:T(128)S(1)}, s32[56]{0:T(128)}, u32[]{:S(2)}) copy-start(s32[56]{0:T(128)} %param.11) | copy-start | bytes 676
  7.7 43.8 %collective-permute-start.2 = (f32[6,32,3,360]{3,1,2,0:T(8,128)}, f32[6,32,3,360]{3,1,2,0:T(8,128)}, u32[]{:S(2)}, u32[]{:S(2)}) collective-permute-start(f32[6,32,3,360]{3,1,2,0:T(8,128)} %copy.65), channel_id=1, source_target_pairs={{8,0},{16,8},{24,16},{32,24},{40,32},{48,40},{56,48},{64,56},{72,6... | collective-permute-start | bytes 2488328 | tf_op jit(solution)/shard_map/ppermute | solution.py:22
  10.5 11.1 %collective-permute-start.1 = (f32[6,32,16,3]{1,2,3,0:T(8,128)S(1)}, f32[6,32,16,3]{1,2,3,0:T(8,128)S(1)}, u32[]{:S(2)}, u32[]{:S(2)}) collective-permute-start(f32[6,32,16,3]{1,2,3,0:T(8,128)S(1)} %copy.64), channel_id=1, source_target_pairs={{0,1},{1,2},{2,3},{3,4},{4,5},{5,6},{6,7},{7,0},{8,9},{9,10},{10,1... | collective-permute-start | bytes 110600 | tf_op jit(solution)/shard_map/ppermute | solution.py:20
  12.8 8.0 %collective-permute-start = (f32[6,32,16,3]{1,2,3,0:T(8,128)S(1)}, f32[6,32,16,3]{1,2,3,0:T(8,128)S(1)}, u32[]{:S(2)}, u32[]{:S(2)}) collective-permute-start(f32[6,32,16,3]{1,2,3,0:T(8,128)S(1)} %copy.63), channel_id=1, source_target_pairs={{1,0},{2,1},{3,2},{4,3},{5,4},{6,5},{7,6},{0,7},{9,8},{10,9},{11,1... | collective-permute-start | bytes 110600 | tf_op jit(solution)/shard_map/ppermute | solution.py:22
  21.5 32.9 %slice-start = ((s8[4718592]{0:T(1024)(128)(4,1)}), s8[524288]{0:T(1024)(128)(4,1)S(1)}, s32[]{:S(2)}) async-start(s8[4718592]{0:T(1024)(128)(4,1)} %bitcast.29), calls=%async_computation.2 | async-start | bytes 1048576
  23.5 31.0 %slice-start.1 = ((s8[4718592]{0:T(1024)(128)(4,1)}), s8[4194304]{0:T(1024)(128)(4,1)S(1)}, s32[]{:S(2)}) async-start(s8[4718592]{0:T(1024)(128)(4,1)} %bitcast.29), calls=%async_computation.3 | async-start | bytes 8388608
  66.7 10.8 %copy-start.4 = (f32[6,6]{1,0:T(8,128)S(1)}, f32[6,6]{1,0:T(8,128)}, u32[]{:S(2)}) copy-start(f32[6,6]{1,0:T(8,128)} %param.8) | copy-start | bytes 436
  91.8 2.7 copy-start.3
  105.4 67.4 %all-to-all-start = ((f32[8,336,360]{2,1,0:T(8,128)}), f32[8,336,360]{2,1,0:T(8,128)}, u32[]{:S(2)}, u32[]{:S(2)}) async-start(f32[8,336,360]{2,1,0:T(8,128)} %all_to_all.26), calls=%async_computation | async-start | bytes 8257536 | tf_op jit(solution)/shard_map/all_to_all | solution.py:76
  178.3 38.6 %slice-start.4 = ((s8[11796480]{0:T(1024)(128)(4,1)}), s8[3407872]{0:T(1024)(128)(4,1)S(1)}, s32[]{:S(2)}) async-start(s8[11796480]{0:T(1024)(128)(4,1)} %bitcast.33), calls=%async_computation.6 | async-start | bytes 6815744
  183.6 33.3 %slice-start.5 = ((s8[11796480]{0:T(1024)(128)(4,1)}), s8[4194304]{0:T(1024)(128)(4,1)S(1)}, s32[]{:S(2)}) async-start(s8[11796480]{0:T(1024)(128)(4,1)} %bitcast.33), calls=%async_computation.7 | async-start | bytes 8388608
  183.6 33.3 %slice-start.6 = ((s8[11796480]{0:T(1024)(128)(4,1)}), s8[4194304]{0:T(1024)(128)(4,1)S(1)}, s32[]{:S(2)}) async-start(s8[11796480]{0:T(1024)(128)(4,1)} %bitcast.33), calls=%async_computation.8 | async-start | bytes 8388608
  259.4 66.0 %all-to-all-start.1 = ((f32[336,8,360]{2,0,1:T(8,128)}), f32[336,8,360]{2,0,1:T(8,128)}, u32[]{:S(2)}, u32[]{:S(2)}) async-start(f32[336,8,360]{2,0,1:T(8,128)} %copy.54), calls=%async_computation.1 | async-start | bytes 8257536 | tf_op jit(solution)/shard_map/all_to_all | solution.py:91
  325.4 11.1 %slice-start.2 = ((s8[6291456]{0:T(1024)(128)(4,1)}), s8[2097152]{0:T(1024)(128)(4,1)S(1)}, s32[]{:S(2)}) async-start(s8[6291456]{0:T(1024)(128)(4,1)} %bitcast.31), calls=%async_computation.4 | async-start | bytes 4194304
  330.5 6.1 %slice-start.3 = ((s8[6291456]{0:T(1024)(128)(4,1)}), s8[4194304]{0:T(1024)(128)(4,1)S(1)}, s32[]{:S(2)}) async-start(s8[6291456]{0:T(1024)(128)(4,1)} %bitcast.31), calls=%async_computation.5 | async-start | bytes 8388608
  336.6 6.2 %copy-start.1 = (f32[6,6]{1,0:T(8,128)S(1)}, f32[6,6]{1,0:T(8,128)}, u32[]{:S(2)}) copy-start(f32[6,6]{1,0:T(8,128)} %param.9) | copy-start | bytes 436
where the time goes:
time: 348 us; the launch traced here: 343 us
  matrix products  102 us (29%)
  other arithmetic  92.8 us (27%)
  waiting for transfers between devices  79.1 us (23%)
  local copies, waits for them, and re-layouts  51.6 us (15%)
  starting transfers between devices  16.7 us (5%)
    all_to_all x1, waiting for transfers between devices, polar_filter(): lax.all_to_all(smoothed, 'lon', split_axis=1, concat_axis=0, tiled=True)  60.3 us
    sin x1, other arithmetic, fourier_table(): return jnp.concatenate([jnp.cos(phase), jnp.sin(phase)], axis=1)  50.4 us
    dot_general x1, matrix products, polar_filter(): jnp.dot(gathered, table, precision=lax.Precision.HIGHEST, preferred_eleme...  33.3 us
    dot_general x1, matrix products, polar_filter(): jnp.einsum('ik,nk->in', weighted, table, precision=lax.Precision.HIGHEST)  31.8 us
    mul x2, other arithmetic, local(): difference(padded_lon, 3, fields.shape[3]) * inv_cos[None, None, :, None]  26.3 us
    all_to_all x3, local copies, waits for them, and re-layouts, polar_filter(): lax.all_to_all(item_rows, 'lon', split_axis=0, concat_axis=1, tiled=True)  15.7 us
    dot_general x1, matrix products, local(): jnp.einsum('fg,glrn->flrn', coupling_lon, along_lon, precision=lax.Precis...  14.3 us
    div x1, other arithmetic, difference(): (45.0 * (shifted(1) - shifted(-1)) - 9.0 * (shifted(2) - shifted(-2)) + (...  12.2 us
  transfers between devices with their start and end apart: 6, of which 3 were waited for; matrix products, arithmetic and copies ran while one was open for 25% of the time, Pallas kernels for 0%

commit v1 on v0

v1 whole, which is shorter than its diff:
```python
import math

import jax
import jax.numpy as jnp
import ml_dtypes
import numpy as np
from jax import lax
from jax.experimental import pallas as pl
from jax.experimental.pallas import tpu as pltpu
from jax.sharding import PartitionSpec as P

MESH = pl.DeviceIdType.MESH
F, LEV, ROWS, CELLS, WIDE = 6, 32, 16, 360, 384
PARTS, LENGTH, KMAX, CAP = 8, 2880, 1024, 14
GROUPS, QUADS = LEV // 8, LEV // 8 * F
SLOT = QUADS
UNITS = CAP * SLOT
REL, OWN = 10, 11
UP0, DOWN0, OWN0 = 0, PARTS * REL, 2 * PARTS * REL
BLOCK = 12
BATCH = 8 * BLOCK
HALF = 1.0 / math.sqrt(2.0)


def tables():
    cells = np.arange(CELLS, dtype=np.int64)

    def angles(waves):
        return 2.0 * np.pi * ((cells[:, None] * waves[None, :]) % LENGTH) / LENGTH

    def halves(table):
        wide = np.asarray(table, np.float64)
        head = wide.astype(ml_dtypes.bfloat16)
        return head, (wide - head.astype(np.float64)).astype(ml_dtypes.bfloat16)

    pair = np.zeros((3, 2 * WIDE, 512))
    single = np.zeros((2, WIDE, 256))
    waves_pair = np.zeros((3, 1, 512), np.int32)
    waves_single = np.zeros((2, 1, 256), np.int32)
    for kind in (1, 2, 3):
        waves = kind + 8 * np.arange(-128, 128)
        cos, sin = np.cos(angles(waves)), np.sin(angles(waves))
        pair[kind - 1, :CELLS, :256] = cos
        pair[kind - 1, :CELLS, 256:] = -sin
        pair[kind - 1, WIDE : WIDE + CELLS, :256] = sin
        pair[kind - 1, WIDE : WIDE + CELLS, 256:] = cos
        waves_pair[kind - 1, 0] = np.concatenate([np.abs(waves)] * 2)
    for at, kind in enumerate((0, 4)):
        waves = kind + 8 * np.arange(128)
        single[at, :CELLS, :128] = np.cos(angles(waves))
        single[at, :CELLS, 128:] = -np.sin(angles(waves))
        waves_single[at, 0] = np.concatenate([waves] * 2)
    return (*halves(pair), *halves(single), waves_pair, waves_single)


def kernel(
    fields, inv_cos, c_lon, c_lat, polar_rows, bands, pair_hi, pair_lo, one_hi, one_lo, waves_pair, waves_one,
    out,
    grid, lon_out, lon_in, pred, slots, relay, pieces, result, back, spec, t_ph, t_pl, t_oh, t_ol, turned,
    tab_sem, lon_ss, lon_rs, lat_ss, lat_rs, help_ss, help_rs, own_ss, own_rs, self_sem, ret_ss, ret_rs, ret_self,
):
    t, i = lax.axis_index("lat"), lax.axis_index("lon")
    north, south = t < 2, t >= 14
    polar = north | south
    up = (t >= 2) & (t < 6)
    down = (t >= 10) & (t < 14)
    helper = up | down
    host = jnp.where(polar, t, jnp.where(up, lax.rem(t + 12, 16), lax.rem(t + 4, 16)))
    flip = host >= 14
    first = jnp.where(host < 2, host, jnp.where(flip, host - 12, 0)) * CAP

    loads = [
        pltpu.make_async_copy(src, dst, tab_sem.at[n])
        for n, (src, dst) in enumerate(((pair_hi, t_ph), (pair_lo, t_pl), (one_hi, t_oh), (one_lo, t_ol)))
    ]
    for load in loads:
        load.start()

    barrier = pltpu.get_barrier_semaphore()

    def greet(lat, lon):
        pl.semaphore_signal(barrier, inc=1, device_id=(lat, lon), device_id_type=MESH)

    for k in range(1, PARTS):
        greet(t, lax.rem(i + k, PARTS))

    @pl.when(t > 0)
    def _():
        greet(t - 1, i)

    @pl.when(t < 15)
    def _():
        greet(t + 1, i)

    @pl.when(polar)
    def _():
        for k in range(PARTS):
            greet(lax.rem(t + 4, 16), k)
            greet(lax.rem(t + 12, 16), k)

    @pl.when(helper)
    def _():
        for k in range(PARTS):
            greet(host, k)

    lane = lax.broadcasted_iota(jnp.int32, (8, 128), 1)

    def turn(at, _):
        f, g = at // GROUPS, lax.rem(at, GROUPS)
        base = pl.multiple_of(at * 128, 128)
        turned[0, pl.ds(base, 128), :] = fields[pl.ds(base, 128), 0:128]
        turned[1, pl.ds(base, 128), :] = fields[pl.ds(base, 128), 128:256]
        turned[2, pl.ds(base, 128), 0 : CELLS - 256] = fields[pl.ds(base, 128), 256:CELLS]
        for r in range(ROWS):
            for c in range(3):
                tile = turned[c, pl.ds(base + r, 8, stride=ROWS), :]
                if c == 2:
                    tile = jnp.where(lane < CELLS - 256, tile, 0.0)
                grid[r + 3, g, f, :, 128 * c : 128 * (c + 1)] = tile
        return 0

    lax.fori_loop(0, QUADS, turn, 0)

    def pack(g, _):
        for pair in range(F // 2):

            def add(r, sums):
                low, high = sums
                for odd in range(2):
                    k = odd * 16 + r
                    mine = lane // 4 == k
                    head = grid[r + 3, g, 2 * pair + odd, :, 0:128]
                    tail = grid[r + 3, g, 2 * pair + odd, :, 256:WIDE]
                    low = jnp.where(mine, pltpu.roll(head, 4 * k, axis=1), low)
                    high = jnp.where(mine, pltpu.roll(tail, lax.rem(4 * k + 128 - 101, 128), axis=1), high)
                return low, high

            zero = jnp.zeros((8, 128), jnp.float32)
            low, high = lax.fori_loop(0, ROWS, add, (zero, zero))
            lon_out[0, g, pair] = low
            lon_out[1, g, pair] = high
        return 0

    lax.fori_loop(0, GROUPS, pack, 0)

    edge = jnp.where(t > 0, 1, 0) + jnp.where(t < 15, 1, 0)
    pl.semaphore_wait(barrier, PARTS - 1 + edge + jnp.where(polar, 2 * PARTS, 0) + jnp.where(helper, PARTS, 0))

    lon_copies = [
        pltpu.make_async_remote_copy(
            src_ref=lon_out.at[side], dst_ref=lon_in.at[side], send_sem=lon_ss.at[side], recv_sem=lon_rs.at[side],
            device_id=(t, lax.rem(i + shift, PARTS)), device_id_type=MESH,
        )
        for side, shift in ((0, PARTS - 1), (1, 1))
    ]
    for copy in lon_copies:
        copy.start()
    south_copy = pltpu.make_async_remote_copy(
        src_ref=grid.at[pl.ds(16, 3)], dst_ref=grid.at[pl.ds(0, 3)], send_sem=lat_ss.at[0], recv_sem=lat_rs.at[0],
        device_id=(jnp.minimum(t + 1, 15), i), device_id_type=MESH,
    )
    north_copy = pltpu.make_async_remote_copy(
        src_ref=grid.at[pl.ds(3, 3)], dst_ref=grid.at[pl.ds(19, 3)], send_sem=lat_ss.at[1], recv_sem=lat_rs.at[1],
        device_id=(jnp.maximum(t - 1, 0), i), device_id_type=MESH,
    )

    @pl.when(t < 15)
    def _():
        south_copy.start()

    @pl.when(t > 0)
    def _():
        north_copy.start()

    def clear(row0):
        def one(r, _):
            for g in range(GROUPS):
                for f in range(F):
                    grid[row0 + r, g, f] = jnp.zeros((8, WIDE), jnp.float32)
            return 0

        lax.fori_loop(0, 3, one, 0)

    @pl.when(t == 0)
    def _():
        clear(0)

    @pl.when(t == 15)
    def _():
        clear(19)

    for copy in lon_copies:
        copy.wait_recv()

    def wait_above():
        @pl.when(t > 0)
        def _():
            south_copy.wait_recv()

    def wait_below():
        @pl.when(t < 15)
        def _():
            north_copy.wait_recv()

    def step(at, _):
        n, g = at // GROUPS, lax.rem(at, GROUPS)
        r = jnp.where(flip, ROWS - 1 - n, n)
        scale = inv_cos[r] * (1.0 / 60.0)
        centre, along_lon, along_lat = [], [], []
        for f in range(F):
            k = (f % 2) * 16 + r
            east = pltpu.roll(lon_in[0, g, f // 2], lax.rem(104 + 128 - 4 * k, 128), axis=1)
            west = pltpu.roll(lon_in[1, g, f // 2], lax.rem(125 + 128 - 4 * k, 128), axis=1)
            mid = grid[r + 3, g, f]
            halo = jnp.where((lane >= 104) & (lane < 107), east, jnp.where(lane >= 125, west, 0.0))
            cells = jnp.concatenate([mid[:, :256], mid[:, 256:] + halo], axis=1)
            centre.append(mid)

            def at_cell(d):
                return pltpu.roll(cells, (WIDE - d) % WIDE, axis=1)

            along_lon.append(
                (45.0 * (at_cell(1) - at_cell(-1)) - 9.0 * (at_cell(2) - at_cell(-2)) + (at_cell(3) - at_cell(-3)))
                * scale
            )

            def at_row(d):
                return grid[r + 3 + d, g, f]

            along_lat.append(
                (45.0 * (at_row(1) - at_row(-1)) - 9.0 * (at_row(2) - at_row(-2)) + (at_row(3) - at_row(-3)))
                * (1.0 / 60.0)
            )
        for f in range(F):
            total = centre[f]
            for h in range(F):
                total = total + c_lon[f * F + h] * along_lon[h] + c_lat[f * F + h] * along_lat[h]
            pred[r, g * F + f] = jnp.where(lax.broadcasted_iota(jnp.int32, (8, WIDE), 1) < CELLS, total, 0.0)

        @pl.when(polar & (g == GROUPS - 1) & (n >= 2))
        def _():
            s = jnp.where(flip, CAP - 1 - (n - 2), n - 2)
            row = jnp.clip(polar_rows[first + s] - t * ROWS, 0, ROWS - 1)
            for q in range(SLOT):
                slots[(n - 2) * SLOT + q] = pred[row, q]

        return 0

    def rows_from(lo, hi):
        lax.fori_loop(lo * GROUPS, hi * GROUPS, step, 0)

    def helper_send(which, j):
        base = (UP0, DOWN0)[which]
        return pltpu.make_async_remote_copy(
            src_ref=slots.at[pl.ds(base + j * REL, REL)], dst_ref=relay.at[j],
            send_sem=help_ss.at[which, j], recv_sem=help_rs.at[j],
            device_id=(lax.rem(t + (4, 12)[which], 16), i), device_id_type=MESH,
        )

    def own_send(block, p, j):
        return pltpu.make_async_remote_copy(
            src_ref=slots.at[pl.ds(OWN0 + block * PARTS * OWN + j * OWN, OWN)],
            dst_ref=pieces.at[block, p, pl.ds(0, OWN)],
            send_sem=own_ss.at[block, j], recv_sem=own_rs.at[block, p],
            device_id=(t, j), device_id_type=MESH,
        )

    def own_local(block):
        return pltpu.make_async_copy(
            slots.at[pl.ds(OWN0 + block * PARTS * OWN + i * OWN, OWN)],
            pieces.at[block, i, pl.ds(0, OWN)], self_sem.at[block],
        )

    def relay_send(p, j):
        return pltpu.make_async_remote_copy(
            src_ref=relay.at[j], dst_ref=pieces.at[0, p, pl.ds(0, REL)],
            send_sem=own_ss.at[0, j], recv_sem=own_rs.at[0, p],
            device_id=(t, j), device_id_type=MESH,
        )

    def relay_local():
        return pltpu.make_async_copy(relay.at[i], pieces.at[0, i, pl.ds(0, REL)], self_sem.at[0])

    @pl.when(polar & jnp.logical_not(flip))
    def _():
        wait_above()

    @pl.when(polar & flip)
    def _():
        wait_below()

    rows_from(jnp.where(polar, 0, 3), 6)

    def others(act):
        def one(k, _):
            act(lax.rem(i + k, PARTS))
            return 0

        lax.fori_loop(1, PARTS, one, 0)

    def everyone(act):
        def one(k, _):
            act(lax.rem(i + k, PARTS))
            return 0

        lax.fori_loop(1, PARTS + 1, one, 0)

    @pl.when(polar)
    def _():
        everyone(lambda j: helper_send(0, j).start())

    rows_from(6, 9)

    @pl.when(polar)
    def _():
        everyone(lambda j: helper_send(1, j).start())

    rows_from(9, 13)

    @pl.when(polar)
    def _():
        others(lambda j: own_send(0, i, j).start())
        own_local(0).start()

    @pl.when(helper)
    def _():
        def pass_on(j):
            helper_send(0, j).wait_recv()
            relay_send(i, j).start()

        others(pass_on)
        helper_send(0, i).wait_recv()
        relay_local().start()

    @pl.when(polar & jnp.logical_not(flip))
    def _():
        wait_below()

    @pl.when(polar & flip)
    def _():
        wait_above()

    @pl.when(jnp.logical_not(polar))
    def _():
        wait_above()
        wait_below()

    rows_from(0, jnp.where(polar, 0, 3))
    rows_from(13, 16)

    @pl.when(polar)
    def _():
        others(lambda j: own_send(1, i, j).start())
        own_local(1).start()

    for load in loads:
        load.wait()

    def ret_own(block, p, j):
        return pltpu.make_async_remote_copy(
            src_ref=result.at[block, p, pl.ds(0, OWN)],
            dst_ref=back.at[pl.ds(OWN0 + block * PARTS * OWN + j * OWN, OWN)],
            send_sem=ret_ss.at[block, p], recv_sem=ret_rs.at[block * PARTS + j],
            device_id=(t, p), device_id_type=MESH,
        )

    def ret_own_local(block):
        return pltpu.make_async_copy(
            result.at[block, i, pl.ds(0, OWN)],
            back.at[pl.ds(OWN0 + block * PARTS * OWN + i * OWN, OWN)], ret_self.at[block],
        )

    def ret_help(which, p, j):
        return pltpu.make_async_remote_copy(
            src_ref=result.at[0, p, pl.ds(0, REL)],
            dst_ref=back.at[pl.ds(which * PARTS * REL + j * REL, REL)],
            send_sem=ret_ss.at[0, p], recv_sem=ret_rs.at[(2 + which) * PARTS + j],
            device_id=(host, p), device_id_type=MESH,
        )

    def matmul(wide, head, tail, back_again):
        top = wide.astype(jnp.bfloat16)
        low = (wide - top.astype(jnp.float32)).astype(jnp.bfloat16)
        dims = (((1,), (1 if back_again else 0,)), ((), ()))
        both = lax.dot_general(
            jnp.concatenate([top, low], axis=0), head, dims, preferred_element_type=jnp.float32
        )
        cross = lax.dot_general(top, tail, dims, preferred_element_type=jnp.float32)
        return both[:BATCH] + (both[BATCH:] + cross)

    def band_column(block):
        start = jnp.where(
            polar,
            OWN0 + block * PARTS * OWN + i * OWN,
            jnp.where(up, UP0 + i * REL, DOWN0 + i * REL),
        )
        unit_of = lax.broadcasted_iota(jnp.int32, (BATCH, 1), 0) // 8
        column = jnp.zeros((BATCH, 1), jnp.int32)
        for n in range(BLOCK):
            s = jnp.minimum((start + n) // SLOT, CAP - 1)
            s = jnp.where(flip, CAP - 1 - s, s)
            column = jnp.where(unit_of == n, bands[first + s], column)
        return column

    def filter_block(block, _):
        @pl.when(polar)
        def _():
            others(lambda p: own_send(block, p, i).wait_recv())
            own_local(block).wait()

        @pl.when(helper)
        def _():
            others(lambda p: relay_send(p, i).wait_recv())
            relay_local().wait()

        def forward(n, _):
            x = [pieces[block, p, n] for p in range(PARTS)]
            e = [x[p] + x[p + 4] for p in range(4)]
            d = [x[p] - x[p + 4] for p in range(4)]
            here = pl.ds(pl.multiple_of(n * 8, 8), 8)
            minus, plus = HALF * (d[1] - d[3]), HALF * (d[1] + d[3])
            parts = (
                d[0] + minus, -plus - d[2],
                e[0] - e[2], e[3] - e[1],
                d[0] - minus, d[2] - plus,
                (e[0] + e[2]) + (e[1] + e[3]), (e[0] + e[2]) - (e[1] + e[3]),
            )
            for m, part in enumerate(parts):
                spec[here, m * WIDE : (m + 1) * WIDE] = part
            return 0

        lax.fori_loop(0, BLOCK, forward, 0)
        column = band_column(block)
        for m in range(3):
            here = slice(m * 2 * WIDE, (m + 1) * 2 * WIDE)
            waves = matmul(spec[:, here], t_ph[m], t_pl[m], False)
            waves = jnp.where(waves_pair[m] < column, waves * (2.0 / LENGTH), 0.0)
            spec[:, here] = matmul(waves, t_ph[m], t_pl[m], True)
        for m in range(2):
            here = slice((6 + m) * WIDE, (7 + m) * WIDE)
            waves = matmul(spec[:, here], t_oh[m], t_ol[m], False)
            factor = jnp.where(waves_one[m] == 0, 1.0 / LENGTH, 2.0 / LENGTH)
            waves = jnp.where(waves_one[m] < column, waves * factor, 0.0)
            spec[:, here] = matmul(waves, t_oh[m], t_ol[m], True)

        def inverse(n, _):
            here = pl.ds(pl.multiple_of(n * 8, 8), 8)
            r1, i1, r2, i2, r3, i3, z0, z4 = (spec[here, m * WIDE : (m + 1) * WIDE] for m in range(8))
            even, odd = z0 + z4, z0 - z4
            a, b = even + r2, even - r2
            c, d = odd - i2, odd + i2
            rr, ii = r1 + r3, i1 - i3
            u = HALF * ((r1 - r3) - (i1 + i3))
            v = HALF * ((r3 - r1) - (i1 + i3))
            outs = (a + rr, c + u, b - ii, d + v, a - rr, c - u, b + ii, d - v)
            for p, value in enumerate(outs):
                result[block, p, n] = value
            return 0

        lax.fori_loop(0, BLOCK, inverse, 0)

        @pl.when(polar)
        def _():
            others(lambda p: ret_own(block, p, i).start())
            ret_own_local(block).start()

        @pl.when(up)
        def _():
            everyone(lambda p: ret_help(0, p, i).start())

        @pl.when(down)
        def _():
            everyone(lambda p: ret_help(1, p, i).start())

        return 0

    lax.fori_loop(0, jnp.where(polar, 2, jnp.where(helper, 1, 0)), filter_block, 0)

    for copy in lon_copies:
        copy.wait_send()

    @pl.when(t < 15)
    def _():
        south_copy.wait_send()

    @pl.when(t > 0)
    def _():
        north_copy.wait_send()

    def put(value_of):
        def one(at, _):
            f, g = at // GROUPS, lax.rem(at, GROUPS)
            base = pl.multiple_of(at * 128, 128)
            for r in range(ROWS):
                value = value_of(r, g * F + f)
                for c in range(3):
                    turned[c, pl.ds(base + r, 8, stride=ROWS), :] = value[:, 128 * c : 128 * (c + 1)]
            out[pl.ds(base, 128), 0:128] = turned[0, pl.ds(base, 128), :]
            out[pl.ds(base, 128), 128:256] = turned[1, pl.ds(base, 128), :]
            out[pl.ds(base, 128), 256:CELLS] = turned[2, pl.ds(base, 128), 0 : CELLS - 256]
            return 0

        lax.fori_loop(0, QUADS, one, 0)

    @pl.when(jnp.logical_not(polar))
    def _():
        put(lambda r, q: pred[r, q])

    @pl.when(helper)
    def _():
        others(lambda j: relay_send(i, j).wait_send())
        everyone(lambda p: ret_help(0, p, i).wait_send())

    @pl.when(polar)
    def _():
        for which in range(2):
            everyone(lambda j: helper_send(which, j).wait_send())
        for block in range(2):
            others(lambda j: own_send(block, i, j).wait_send())
            others(lambda p: ret_own(block, p, i).wait_send())
            others(lambda j: ret_own(block, i, j).wait_recv())
            ret_own_local(block).wait()
        for which in range(2):
            everyone(lambda j: ret_help(which, i, j).wait_recv())

        place = []
        for r in range(ROWS):
            before, hit = 0, 0
            for s in range(CAP):
                row = polar_rows[first + s] - t * ROWS
                before = before + jnp.where(row < r, 1, 0)
                hit = hit + jnp.where(row == r, 1, 0)
            s = jnp.minimum(before, CAP - 1)
            place.append((hit > 0, jnp.where(flip, CAP - 1 - s, s) * SLOT))
        put(lambda r, q: jnp.where(place[r][0], back[place[r][1] + q], pred[r, q]))


def local(fields, inv_cos, coupling_lon, coupling_lat, polar_rows, bands):
    smem, vmem, anywhere = (pl.BlockSpec(memory_space=space) for space in (pltpu.SMEM, pltpu.VMEM, pl.ANY))
    dma = pltpu.SemaphoreType.DMA
    pair_hi, pair_lo, one_hi, one_lo, waves_pair, waves_one = tables()
    f32, bf16 = jnp.float32, jnp.bfloat16
    out = pl.pallas_call(
        kernel,
        out_shape=jax.ShapeDtypeStruct((F * LEV * ROWS, CELLS), f32),
        in_specs=[vmem] + [smem] * 5 + [anywhere] * 4 + [vmem] * 2,
        out_specs=vmem,
        scratch_shapes=[
            pltpu.VMEM((ROWS + 6, GROUPS, F, 8, WIDE), f32),
            pltpu.VMEM((2, GROUPS, F // 2, 8, 128), f32),
            pltpu.VMEM((2, GROUPS, F // 2, 8, 128), f32),
            pltpu.VMEM((ROWS, QUADS, 8, WIDE), f32),
            pltpu.VMEM((UNITS, 8, WIDE), f32),
            pltpu.VMEM((PARTS, REL, 8, WIDE), f32),
            pltpu.VMEM((2, PARTS, BLOCK, 8, WIDE), f32),
            pltpu.VMEM((2, PARTS, BLOCK, 8, WIDE), f32),
            pltpu.VMEM((UNITS, 8, WIDE), f32),
            pltpu.VMEM((BATCH, 8 * WIDE), f32),
            pltpu.VMEM((3, 2 * WIDE, 512), bf16),
            pltpu.VMEM((3, 2 * WIDE, 512), bf16),
            pltpu.VMEM((2, WIDE, 256), bf16),
            pltpu.VMEM((2, WIDE, 256), bf16),
            pltpu.VMEM((3, F * LEV * ROWS, 128), f32),
            dma((4,)),
            dma((2,)), dma((2,)), dma((2,)), dma((2,)),
            dma((2, PARTS)), dma((PARTS,)),
            dma((2, PARTS)), dma((2, PARTS)), dma((2,)),
            dma((2, PARTS)), dma((4 * PARTS,)), dma((2,)),
        ],
        compiler_params=pltpu.CompilerParams(
            collective_id=0, has_side_effects=True, vmem_limit_bytes=60 * 2**20
        ),
    )(
        fields.reshape(F * LEV * ROWS, CELLS),
        inv_cos,
        coupling_lon.reshape(-1),
        coupling_lat.reshape(-1),
        polar_rows,
        bands,
        jnp.asarray(pair_hi), jnp.asarray(pair_lo), jnp.asarray(one_hi), jnp.asarray(one_lo),
        jnp.asarray(waves_pair), jnp.asarray(waves_one),
    )
    return out.reshape(F, LEV, ROWS, CELLS)


def solution(mesh):
    return jax.shard_map(
        local,
        mesh=mesh,
        in_specs=(P(None, None, "lat", "lon"), P("lat"), P(), P(), P(), P()),
        out_specs=P(None, None, "lat", "lon"),
        check_vma=False,
    )
```

time: 348 us -> 106 us (0.30)
  the two profiles are of different devices: /device:TPU:6 before, /device:TPU:0 now
where the time goes in v1:
time: 106 us; the launch traced here: 104 us
  Pallas kernels  96.7 us (91%)
  local copies, waits for them, and re-layouts  7.61 us (7%)
    pallas_call x1, Pallas kernels, local(): pl.pallas_call(kernel, out_shape=jax.ShapeDtypeStruct((F * LEV * ROWS, CE...  96.7 us
    unnamed x1, local copies, waits for them, and re-layouts  5.1 us

profile of v1, /device:TPU:0, one launch (start us, length us, event | category | flops | bytes accessed | tf_op | source)
XLA Modules:
  0.0 104.3 jit_solution(11364233819076596445)
XLA Ops:
  0.0 1.3 %reshape.13.c_lon = f32[36]{0:T(128)} reshape(f32[6,6]{1,0:T(8,128)} %param.14) | data formatting | bytes 288 | tf_op jit(solution)/shard_map/reshape | solution.py:576
  1.3 1.2 %reshape.14.c_lat = f32[36]{0:T(128)} reshape(f32[6,6]{1,0:T(8,128)} %param.15) | data formatting | bytes 288 | tf_op jit(solution)/shard_map/reshape | solution.py:577
  2.5 96.7 %shard_map.118 = f32[3072,360]{1,0:T(8,128)} custom-call(f32[3072,360]{1,0:T(8,128)} %bitcast.3, f32[16]{0:T(128)} %inv_cos.1, f32[36]{0:T(128)} %reshape.13.c_lon, f32[36]{0:T(128)} %reshape.14.c_lat, s32[56]{0:T(128)} %polar_rows.1, s32[56]{0:T(128)} %bands.1, bf16[3,768,512]{2,1,0:T(8,128)(2,1)} %constant.12.clone.pair_hi, ...), custom_call_target="tpu_custom_call" | custom-call | tf_op jit(solution)/shard_map/pallas_call | solution.py:543
  99.2 5.1 %copy.14 = f32[6,32,16,360]{3,2,1,0:T(8,128)} copy(f32[6,32,16,360]{3,2,1,0:T(8,128)} %bitcast.2) | data formatting | bytes 8847360

commit v2 on v1

--- a/solution.py
+++ b/solution.py
@@ -1,3 +1,4 @@
+import functools
 import math
 
 import jax
@@ -15,9 +16,10 @@
 GROUPS, QUADS = LEV // 8, LEV // 8 * F
 SLOT = QUADS
 UNITS = CAP * SLOT
-REL, OWN = 10, 11
-UP0, DOWN0, OWN0 = 0, PARTS * REL, 2 * PARTS * REL
-BLOCK = 12
+BLOCK = 6
+SEGMENT = PARTS * BLOCK
+HELP_SEGMENTS = ((0, 3), (1, 4))
+OWN_SEGMENTS = (2, 5, 6)
 BATCH = 8 * BLOCK
 HALF = 1.0 / math.sqrt(2.0)
 
@@ -55,8 +57,8 @@
 
 def kernel(
     fields, inv_cos, c_lon, c_lat, polar_rows, bands, pair_hi, pair_lo, one_hi, one_lo, waves_pair, waves_one,
-    out,
-    grid, lon_out, lon_in, pred, slots, relay, pieces, result, back, spec, t_ph, t_pl, t_oh, t_ol, turned,
+    pred, back,
+    grid, lon_out, lon_in, slots, relay, pieces, result, spec, t_ph, t_pl, t_oh, t_ol, turned,
     tab_sem, lon_ss, lon_rs, lat_ss, lat_rs, help_ss, help_rs, own_ss, own_rs, self_sem, ret_ss, ret_rs, ret_self,
 ):
     t, i = lax.axis_index("lat"), lax.axis_index("lon")
@@ -106,42 +108,28 @@
     lane = lax.broadcasted_iota(jnp.int32, (8, 128), 1)
 
     def turn(at, _):
-        f, g = at // GROUPS, lax.rem(at, GROUPS)
-        base = pl.multiple_of(at * 128, 128)
-        turned[0, pl.ds(base, 128), :] = fields[pl.ds(base, 128), 0:128]
-        turned[1, pl.ds(base, 128), :] = fields[pl.ds(base, 128), 128:256]
-        turned[2, pl.ds(base, 128), 0 : CELLS - 256] = fields[pl.ds(base, 128), 256:CELLS]
-        for r in range(ROWS):
-            for c in range(3):
-                tile = turned[c, pl.ds(base + r, 8, stride=ROWS), :]
-                if c == 2:
-                    tile = jnp.where(lane < CELLS - 256, tile, 0.0)
-                grid[r + 3, g, f, :, 128 * c : 128 * (c + 1)] = tile
+        g, pair = at // (F // 2), lax.rem(at, F // 2)
+        low, high = [], []
+        for odd in range(2):
+            f = 2 * pair + odd
+            base = pl.multiple_of(f * LEV * ROWS + g * 128, 128)
+            turned[0, odd] = fields[pl.ds(base, 128), 0:128]
+            turned[1, odd] = fields[pl.ds(base, 128), 128:256]
+            turned[2, odd, :, 0 : CELLS - 256] = fields[pl.ds(base, 128), 256:CELLS]
+            for r in range(ROWS):
+                k = odd * 16 + r
+                tiles = [turned[c, odd, pl.ds(r, 8, stride=ROWS), :] for c in range(3)]
+                tiles[2] = jnp.where(lane < CELLS - 256, tiles[2], 0.0)
+                for c in range(3):
+                    grid[r + 3, g, f, :, 128 * c : 128 * (c + 1)] = tiles[c]
+                mine = lane // 4 == k
+                low.append(jnp.where(mine, pltpu.roll(tiles[0], 4 * k, axis=1), 0.0))
+                high.append(jnp.where(mine, pltpu.roll(tiles[2], (4 * k + 128 - 101) % 128, axis=1), 0.0))
+        lon_out[0, g, pair] = functools.reduce(jnp.add, low)
+        lon_out[1, g, pair] = functools.reduce(jnp.add, high)
         return 0
 
-    lax.fori_loop(0, QUADS, turn, 0)
-
-    def pack(g, _):
-        for pair in range(F // 2):
-
-            def add(r, sums):
-                low, high = sums
-                for odd in range(2):
-                    k = odd * 16 + r
-                    mine = lane // 4 == k
-                    head = grid[r + 3, g, 2 * pair + odd, :, 0:128]
-                    tail = grid[r + 3, g, 2 * pair + odd, :, 256:WIDE]
-                    low = jnp.where(mine, pltpu.roll(head, 4 * k, axis=1), low)
-                    high = jnp.where(mine, pltpu.roll(tail, lax.rem(4 * k + 128 - 101, 128), axis=1), high)
-                return low, high
-
-            zero = jnp.zeros((8, 128), jnp.float32)
-            low, high = lax.fori_loop(0, ROWS, add, (zero, zero))
-            lon_out[0, g, pair] = low
-            lon_out[1, g, pair] = high
-        return 0
-
-    lax.fori_loop(0, GROUPS, pack, 0)
+    lax.fori_loop(0, GROUPS * F // 2, turn, 0)
 
     edge = jnp.where(t > 0, 1, 0) + jnp.where(t < 15, 1, 0)
     pl.semaphore_wait(barrier, PARTS - 1 + edge + jnp.where(polar, 2 * PARTS, 0) + jnp.where(helper, PARTS, 0))
@@ -202,8 +190,55 @@
         def _():
             north_copy.wait_recv()
 
+    def others(act):
+        def one(k, _):
+            act(lax.rem(i + k, PARTS))
+            return 0
+
+        lax.fori_loop(1, PARTS, one, 0)
+
+    def everyone(act):
+        others(act)
+        act(i)
+
+    def units(segment, j):
+        return pl.ds(segment * SEGMENT + j * BLOCK, BLOCK)
+
+    def own_segment(block):
+        return jnp.where(block == 0, OWN_SEGMENTS[0], OWN_SEGMENTS[1] - 1 + block)
+
+    def help_send(which, block, j):
+        return pltpu.make_async_remote_copy(
+            src_ref=slots.at[units(HELP_SEGMENTS[which][block], j)], dst_ref=relay.at[block, j],
+            send_sem=help_ss.at[which, block, j], recv_sem=help_rs.at[block, j],
+            device_id=(lax.rem(t + (4, 12)[which], 16), i), device_id_type=MESH,
+        )
+
+    def own_send(block, p, j):
+        return pltpu.make_async_remote_copy(
+            src_ref=slots.at[units(own_segment(block), j)], dst_ref=pieces.at[block, p],
+            send_sem=own_ss.at[block, j], recv_sem=own_rs.at[block, p],
+            device_id=(t, j), device_id_type=MESH,
+        )
+
+    def own_local(block):
+        return pltpu.make_async_copy(
+            slots.at[units(own_segment(block), i)], pieces.at[block, i], self_sem.at[block]
+        )
+
+    def relay_send(block, p, j):
+        return pltpu.make_async_remote_copy(
+            src_ref=relay.at[block, j], dst_ref=pieces.at[block, p],
+            send_sem=own_ss.at[block, j], recv_sem=own_rs.at[block, p],
+            device_id=(t, j), device_id_type=MESH,
+        )
+
+    def relay_local(block):
+        return pltpu.make_async_copy(relay.at[block, i], pieces.at[block, i], self_sem.at[block])
+
     def step(at, _):
         n, g = at // GROUPS, lax.rem(at, GROUPS)
+        n = jnp.where(n < ROWS, n, jnp.where(n < ROWS + 3, n - ROWS, n - 6))
         r = jnp.where(flip, ROWS - 1 - n, n)
         scale = inv_cos[r] * (1.0 / 60.0)
         centre, along_lon, along_lat = [], [], []
@@ -234,7 +269,7 @@
         for f in range(F):
             total = centre[f]
             for h in range(F):
-                total = total + c_lon[f * F + h] * along_lon[h] + c_lat[f * F + h] * along_lat[h]
+                total = total + c_lon[f, h] * along_lon[h] + c_lat[f, h] * along_lat[h]
             pred[r, g * F + f] = jnp.where(lax.broadcasted_iota(jnp.int32, (8, WIDE), 1) < CELLS, total, 0.0)
 
         @pl.when(polar & (g == GROUPS - 1) & (n >= 2))
@@ -244,43 +279,25 @@
             for q in range(SLOT):
                 slots[(n - 2) * SLOT + q] = pred[row, q]
 
+            for which in range(2):
+                for block in range(2):
+
+                    @pl.when(n == 2 * HELP_SEGMENTS[which][block] + 3)
+                    def _():
+                        everyone(lambda j: help_send(which, block, j).start())
+
+            for block, segment in enumerate(OWN_SEGMENTS):
+
+                @pl.when(n == 2 * segment + 3)
+                def _():
+                    others(lambda j: own_send(block, i, j).start())
+                    own_local(block).start()
+
         return 0
 
     def rows_from(lo, hi):
         lax.fori_loop(lo * GROUPS, hi * GROUPS, step, 0)
 
-    def helper_send(which, j):
-        base = (UP0, DOWN0)[which]
-        return pltpu.make_async_remote_copy(
-            src_ref=slots.at[pl.ds(base + j * REL, REL)], dst_ref=relay.at[j],
-            send_sem=help_ss.at[which, j], recv_sem=help_rs.at[j],
-            device_id=(lax.rem(t + (4, 12)[which], 16), i), device_id_type=MESH,
-        )
-
-    def own_send(block, p, j):
-        return pltpu.make_async_remote_copy(
-            src_ref=slots.at[pl.ds(OWN0 + block * PARTS * OWN + j * OWN, OWN)],
-            dst_ref=pieces.at[block, p, pl.ds(0, OWN)],
-            send_sem=own_ss.at[block, j], recv_sem=own_rs.at[block, p],
-            device_id=(t, j), device_id_type=MESH,
-        )
-
-    def own_local(block):
-        return pltpu.make_async_copy(
-            slots.at[pl.ds(OWN0 + block * PARTS * OWN + i * OWN, OWN)],
-            pieces.at[block, i, pl.ds(0, OWN)], self_sem.at[block],
-        )
-
-    def relay_send(p, j):
-        return pltpu.make_async_remote_copy(
-            src_ref=relay.at[j], dst_ref=pieces.at[0, p, pl.ds(0, REL)],
-            send_sem=own_ss.at[0, j], recv_sem=own_rs.at[0, p],
-            device_id=(t, j), device_id_type=MESH,
-        )
-
-    def relay_local():
-        return pltpu.make_async_copy(relay.at[i], pieces.at[0, i, pl.ds(0, REL)], self_sem.at[0])
-
     @pl.when(polar & jnp.logical_not(flip))
     def _():
         wait_above()
@@ -289,92 +306,24 @@
     def _():
         wait_below()
 
-    rows_from(jnp.where(polar, 0, 3), 6)
-
-    def others(act):
-        def one(k, _):
-            act(lax.rem(i + k, PARTS))
-            return 0
-
-        lax.fori_loop(1, PARTS, one, 0)
-
-    def everyone(act):
-        def one(k, _):
-            act(lax.rem(i + k, PARTS))
-            return 0
-
-        lax.fori_loop(1, PARTS + 1, one, 0)
-
-    @pl.when(polar)
-    def _():
-        everyone(lambda j: helper_send(0, j).start())
-
-    rows_from(6, 9)
-
-    @pl.when(polar)
-    def _():
-        everyone(lambda j: helper_send(1, j).start())
-
-    rows_from(9, 13)
-
-    @pl.when(polar)
-    def _():
-        others(lambda j: own_send(0, i, j).start())
-        own_local(0).start()
-
-    @pl.when(helper)
-    def _():
-        def pass_on(j):
-            helper_send(0, j).wait_recv()
-            relay_send(i, j).start()
-
-        others(pass_on)
-        helper_send(0, i).wait_recv()
-        relay_local().start()
-
-    @pl.when(polar & jnp.logical_not(flip))
-    def _():
-        wait_below()
-
-    @pl.when(polar & flip)
-    def _():
-        wait_above()
-
-    @pl.when(jnp.logical_not(polar))
-    def _():
-        wait_above()
-        wait_below()
-
-    rows_from(0, jnp.where(polar, 0, 3))
-    rows_from(13, 16)
-
-    @pl.when(polar)
-    def _():
-        others(lambda j: own_send(1, i, j).start())
-        own_local(1).start()
-
-    for load in loads:
-        load.wait()
+    rows_from(jnp.where(polar, 0, 3), 13)
 
     def ret_own(block, p, j):
         return pltpu.make_async_remote_copy(
-            src_ref=result.at[block, p, pl.ds(0, OWN)],
-            dst_ref=back.at[pl.ds(OWN0 + block * PARTS * OWN + j * OWN, OWN)],
-            send_sem=ret_ss.at[block, p], recv_sem=ret_rs.at[block * PARTS + j],
+            src_ref=result.at[block, p], dst_ref=back.at[units(own_segment(block), j)],
+            send_sem=ret_ss.at[block, p], recv_sem=ret_rs.at[block, j],
             device_id=(t, p), device_id_type=MESH,
         )
 
     def ret_own_local(block):
         return pltpu.make_async_copy(
-            result.at[block, i, pl.ds(0, OWN)],
-            back.at[pl.ds(OWN0 + block * PARTS * OWN + i * OWN, OWN)], ret_self.at[block],
-        )
-
-    def ret_help(which, p, j):
+            result.at[block, i], back.at[units(own_segment(block), i)], ret_self.at[block]
+        )
+
+    def ret_help(which, block, p, j):
         return pltpu.make_async_remote_copy(
-            src_ref=result.at[0, p, pl.ds(0, REL)],
-            dst_ref=back.at[pl.ds(which * PARTS * REL + j * REL, REL)],
-            send_sem=ret_ss.at[0, p], recv_sem=ret_rs.at[(2 + which) * PARTS + j],
+            src_ref=result.at[block, p], dst_ref=back.at[units(3 * block + which, j)],
+            send_sem=ret_ss.at[block, p], recv_sem=ret_rs.at[3 + 2 * which + block, j],
             device_id=(host, p), device_id_type=MESH,
         )
 
@@ -389,11 +338,8 @@
         return both[:BATCH] + (both[BATCH:] + cross)
 
     def band_column(block):
-        start = jnp.where(
-            polar,
-            OWN0 + block * PARTS * OWN + i * OWN,
-            jnp.where(up, UP0 + i * REL, DOWN0 + i * REL),
-        )
+        segment = jnp.where(polar, own_segment(block), 3 * block + jnp.where(up, 0, 1))
+        start = segment * SEGMENT + i * BLOCK
         unit_of = lax.broadcasted_iota(jnp.int32, (BATCH, 1), 0) // 8
         column = jnp.zeros((BATCH, 1), jnp.int32)
         for n in range(BLOCK):
@@ -410,8 +356,8 @@
 
         @pl.when(helper)
         def _():
-            others(lambda p: relay_send(p, i).wait_recv())
-            relay_local().wait()
+            others(lambda p: relay_send(block, p, i).wait_recv())
+            relay_local(block).wait()
 
         def forward(n, _):
             x = [pieces[block, p, n] for p in range(PARTS)]
@@ -466,15 +412,47 @@
 
         @pl.when(up)
         def _():
-            everyone(lambda p: ret_help(0, p, i).start())
+            everyone(lambda p: ret_help(0, block, p, i).start())
 
         @pl.when(down)
         def _():
-            everyone(lambda p: ret_help(1, p, i).start())
+            everyone(lambda p: ret_help(1, block, p, i).start())
 
         return 0
 
-    lax.fori_loop(0, jnp.where(polar, 2, jnp.where(helper, 1, 0)), filter_block, 0)
+    def pass_on(block):
+        @pl.when(helper)
+        def _():
+            def one(j):
+                help_send(0, block, j).wait_recv()
+                relay_send(block, i, j).start()
+
+            others(one)
+            help_send(0, block, i).wait_recv()
+            relay_local(block).start()
+
+    for load in loads:
+        load.wait()
+    pass_on(0)
+    busy = jnp.where(polar | helper, 1, 0)
+    lax.fori_loop(0, busy, filter_block, 0)
+    pass_on(1)
+
+    @pl.when(polar & jnp.logical_not(flip))
+    def _():
+        wait_below()
+
+    @pl.when(polar & flip)
+    def _():
+        wait_above()
+
+    @pl.when(jnp.logical_not(polar))
+    def _():
+        wait_above()
+        wait_below()
+
+    rows_from(ROWS + jnp.where(polar, 3, 0), ROWS + 6)
+    lax.fori_loop(1, jnp.where(polar, 3, jnp.where(helper, 2, 1)), filter_block, 0)
 
     for copy in lon_copies:
         copy.wait_send()
@@ -487,52 +465,47 @@
     def _():
         north_copy.wait_send()
 
-    def put(value_of):
-        def one(at, _):
-            f, g = at // GROUPS, lax.rem(at, GROUPS)
-            base = pl.multiple_of(at * 128, 128)
-            for r in range(ROWS):
-                value = value_of(r, g * F + f)
-                for c in range(3):
-                    turned[c, pl.ds(base + r, 8, stride=ROWS), :] = value[:, 128 * c : 128 * (c + 1)]
-            out[pl.ds(base, 128), 0:128] = turned[0, pl.ds(base, 128), :]
-            out[pl.ds(base, 128), 128:256] = turned[1, pl.ds(base, 128), :]
-            out[pl.ds(base, 128), 256:CELLS] = turned[2, pl.ds(base, 128), 0 : CELLS - 256]
-            return 0
-
-        lax.fori_loop(0, QUADS, one, 0)
-
-    @pl.when(jnp.logical_not(polar))
-    def _():
-        put(lambda r, q: pred[r, q])
-
     @pl.when(helper)
     def _():
-        others(lambda j: relay_send(i, j).wait_send())
-        everyone(lambda p: ret_help(0, p, i).wait_send())
+        for block in range(2):
+            others(lambda j: relay_send(block, i, j).wait_send())
+            everyone(lambda p: ret_help(0, block, p, i).wait_send())
 
     @pl.when(polar)
     def _():
-        for which in range(2):
-            everyone(lambda j: helper_send(which, j).wait_send())
-        for block in range(2):
+        for block in range(3):
             others(lambda j: own_send(block, i, j).wait_send())
             others(lambda p: ret_own(block, p, i).wait_send())
             others(lambda j: ret_own(block, i, j).wait_recv())
             ret_own_local(block).wait()
         for which in range(2):
-            everyone(lambda j: ret_help(which, i, j).wait_recv())
-
-        place = []
+            for block in range(2):
+                everyone(lambda j: help_send(which, block, j).wait_send())
+                everyone(lambda j: ret_help(which, block, i, j).wait_recv())
+
+
+def place(polar_rows, pred, back, out, turned):
+    t = lax.axis_index("lat")
+    polar, flip = (t < 2) | (t >= 14), t >= 14
+    first = jnp.where(t < 2, t, jnp.where(flip, t - 12, 0)) * CAP
+    slot_of = []
+    for r in range(ROWS):
+        before, hit = 0, 0
+        for s in range(CAP):
+            row = polar_rows[first + s] - t * ROWS
+            before = before + jnp.where(row < r, 1, 0)
+            hit = hit + jnp.where(row == r, 1, 0)
+        s = jnp.minimum(before, CAP - 1)
+        slot_of.append((polar & (hit > 0), jnp.where(flip, CAP - 1 - s, s)))
+    for odd in range(2):
         for r in range(ROWS):
-            before, hit = 0, 0
-            for s in range(CAP):
-                row = polar_rows[first + s] - t * ROWS
-                before = before + jnp.where(row < r, 1, 0)
-                hit = hit + jnp.where(row == r, 1, 0)
-            s = jnp.minimum(before, CAP - 1)
-            place.append((hit > 0, jnp.where(flip, CAP - 1 - s, s) * SLOT))
-        put(lambda r, q: jnp.where(place[r][0], back[place[r][1] + q], pred[r, q]))
+            hit, s = slot_of[r]
+            value = jnp.where(hit, back[s, 0, odd], pred[r, 0, odd])
+            for c in range(3):
+                turned[c, odd, pl.ds(r, 8, stride=ROWS), :] = value[:, 128 * c : 128 * (c + 1)]
+        out[odd, 0, :, 0:128] = turned[0, odd]
+        out[odd, 0, :, 128:256] = turned[1, odd]
+        out[odd, 0, :, 256:CELLS] = turned[2, odd, :, 0 : CELLS - 256]
 
 
 def local(fields, inv_cos, coupling_lon, coupling_lat, polar_rows, bands):
@@ -540,32 +513,33 @@
     dma = pltpu.SemaphoreType.DMA
     pair_hi, pair_lo, one_hi, one_lo, waves_pair, waves_one = tables()
     f32, bf16 = jnp.float32, jnp.bfloat16
-    out = pl.pallas_call(
+    pred, back = pl.pallas_call(
         kernel,
-        out_shape=jax.ShapeDtypeStruct((F * LEV * ROWS, CELLS), f32),
+        out_shape=(
+            jax.ShapeDtypeStruct((ROWS, QUADS, 8, WIDE), f32),
+            jax.ShapeDtypeStruct((UNITS, 8, WIDE), f32),
+        ),
         in_specs=[vmem] + [smem] * 5 + [anywhere] * 4 + [vmem] * 2,
-        out_specs=vmem,
+        out_specs=(vmem, vmem),
         scratch_shapes=[
             pltpu.VMEM((ROWS + 6, GROUPS, F, 8, WIDE), f32),
             pltpu.VMEM((2, GROUPS, F // 2, 8, 128), f32),
             pltpu.VMEM((2, GROUPS, F // 2, 8, 128), f32),
-            pltpu.VMEM((ROWS, QUADS, 8, WIDE), f32),
             pltpu.VMEM((UNITS, 8, WIDE), f32),
-            pltpu.VMEM((PARTS, REL, 8, WIDE), f32),
             pltpu.VMEM((2, PARTS, BLOCK, 8, WIDE), f32),
-            pltpu.VMEM((2, PARTS, BLOCK, 8, WIDE), f32),
-            pltpu.VMEM((UNITS, 8, WIDE), f32),
+            pltpu.VMEM((3, PARTS, BLOCK, 8, WIDE), f32),
+            pltpu.VMEM((3, PARTS, BLOCK, 8, WIDE), f32),
             pltpu.VMEM((BATCH, 8 * WIDE), f32),
             pltpu.VMEM((3, 2 * WIDE, 512), bf16),
             pltpu.VMEM((3, 2 * WIDE, 512), bf16),
             pltpu.VMEM((2, WIDE, 256), bf16),
             pltpu.VMEM((2, WIDE, 256), bf16),
-            pltpu.VMEM((3, F * LEV * ROWS, 128), f32),
+            pltpu.VMEM((3, 2, 128, 128), f32),
             dma((4,)),
             dma((2,)), dma((2,)), dma((2,)), dma((2,)),
-            dma((2, PARTS)), dma((PARTS,)),
-            dma((2, PARTS)), dma((2, PARTS)), dma((2,)),
-            dma((2, PARTS)), dma((4 * PARTS,)), dma((2,)),
+            dma((2, 2, PARTS)), dma((2, PARTS)),
+            dma((3, PARTS)), dma((3, PARTS)), dma((3,)),
+            dma((3, PARTS)), dma((7, PARTS)), dma((3,)),
         ],
         compiler_params=pltpu.CompilerParams(
             collective_id=0, has_side_effects=True, vmem_limit_bytes=60 * 2**20
@@ -573,12 +547,28 @@
     )(
         fields.reshape(F * LEV * ROWS, CELLS),
         inv_cos,
-        coupling_lon.reshape(-1),
-        coupling_lat.reshape(-1),
+        coupling_lon,
+        coupling_lat,
         polar_rows,
         bands,
         jnp.asarray(pair_hi), jnp.asarray(pair_lo), jnp.asarray(one_hi), jnp.asarray(one_lo),
         jnp.asarray(waves_pair), jnp.asarray(waves_one),
+    )
+    out = pl.pallas_call(
+        place,
+        grid=(GROUPS, F // 2),
+        out_shape=jax.ShapeDtypeStruct((F, GROUPS, 8 * ROWS, CELLS), f32),
+        in_specs=[
+            smem,
+            pl.BlockSpec((ROWS, 1, 2, 8, WIDE), lambda g, pair: (0, g, pair, 0, 0)),
+            pl.BlockSpec((CAP, 1, 2, 8, WIDE), lambda g, pair: (0, g, pair, 0, 0)),
+        ],
+        out_specs=pl.BlockSpec((2, 1, 8 * ROWS, CELLS), lambda g, pair: (pair, g, 0, 0)),
+        scratch_shapes=[pltpu.VMEM((3, 2, 8 * ROWS, 128), f32)],
+    )(
+        polar_rows,
+        pred.reshape(ROWS, GROUPS, F, 8, WIDE),
+        back.reshape(CAP, GROUPS, F, 8, WIDE),
     )
     return out.reshape(F, LEV, ROWS, CELLS)
 

time: 106 us -> 95.2 us (0.90)
  local copies, waits for them, and re-layouts: 7.61 us -> 0 us
  Pallas kernels: 96.7 us -> 93.9 us
    unnamed x1 -> x0, local copies, waits for them, and re-layouts: 5.1 us -> none
    pallas_call x1 -> x2, Pallas kernels: 96.7 us -> 93.9 us  [the longest x1 80.3 us: local(): pl.pallas_call(kernel, out_shape=(jax.ShapeDtypeStruct((ROWS, QUADS, 8, W...]
    reshape x2 -> x0, local copies, waits for them, and re-layouts: 2.52 us -> none  [the longest x1 1.27 us: local(): coupling_lon.reshape(-1)]
where the time goes in v2:
time: 95.2 us; the launch traced here: 93.9 us
  Pallas kernels  93.9 us (99%)
    pallas_call x1, Pallas kernels, local(): pl.pallas_call(kernel, out_shape=(jax.ShapeDtypeStruct((ROWS, QUADS, 8, W...  80.3 us
    pallas_call x1, Pallas kernels, local(): pl.pallas_call(place, grid=(GROUPS, F // 2), out_shape=jax.ShapeDtypeStru...  13.6 us

profile of v2, /device:TPU:0, one launch (start us, length us, event | category | flops | bytes accessed | tf_op | source)
XLA Modules:
  0.0 93.9 jit_solution(15573646542529613347)
XLA Ops:
  0.0 80.3 %shard_map.118 = (f32[16,24,8,384]{3,2,1,0:T(8,128)}, f32[336,8,384]{2,1,0:T(8,128)}) custom-call(f32[3072,360]{1,0:T(8,128)} %bitcast.4, f32[16]{0:T(128)} %inv_cos.1, f32[6,6]{1,0:T(8,128)} %c_lon.1, f32[6,6]{1,0:T(8,128)} %c_lat.1, s32[56]{0:T(128)} %polar_rows.3, s32[56]{0:T(128)} %bands.1, bf16[3,768,512]{2,1,0:T(8,128)(2,1)} %constant.12.clone.pair_hi, ...), custom_call_target="tpu_custom_call" | custom-call | tf_op jit(solution)/shard_map/pallas_call | solution.py:516
  80.3 13.6 %shard_map.119 = f32[6,4,128,360]{3,2,1,0:T(8,128)} custom-call(s32[56]{0:T(128)} %polar_rows.3, f32[16,4,6,8,384]{4,3,2,1,0:T(8,128)} %bitcast.5, f32[14,4,6,8,384]{4,3,2,1,0:T(8,128)} %bitcast.6), custom_call_target="tpu_custom_call" | custom-call | tf_op jit(solution)/shard_map/pallas_call | solution.py:557

commit v3 on v2

--- a/solution.py
+++ b/solution.py
@@ -484,7 +484,7 @@
                 everyone(lambda j: ret_help(which, block, i, j).wait_recv())
 
 
-def place(polar_rows, pred, back, out, turned):
+def place(polar_rows, pred, back, out, turned, ready, sems):
     t = lax.axis_index("lat")
     polar, flip = (t < 2) | (t >= 14), t >= 14
     first = jnp.where(t < 2, t, jnp.where(flip, t - 12, 0)) * CAP
@@ -497,18 +497,35 @@
             hit = hit + jnp.where(row == r, 1, 0)
         s = jnp.minimum(before, CAP - 1)
         slot_of.append((polar & (hit > 0), jnp.where(flip, CAP - 1 - s, s)))
-    for odd in range(2):
+
+    def leave(at):
+        return pltpu.make_async_copy(ready.at[at], out.at[at], sems.at[at])
+
+    def one(at, _):
+        f, g = at // GROUPS, lax.rem(at, GROUPS)
+        q = g * F + f
         for r in range(ROWS):
             hit, s = slot_of[r]
-            value = jnp.where(hit, back[s, 0, odd], pred[r, 0, odd])
+            value = jnp.where(hit, back[s * SLOT + q], pred[r, q])
             for c in range(3):
-                turned[c, odd, pl.ds(r, 8, stride=ROWS), :] = value[:, 128 * c : 128 * (c + 1)]
-        out[odd, 0, :, 0:128] = turned[0, odd]
-        out[odd, 0, :, 128:256] = turned[1, odd]
-        out[odd, 0, :, 256:CELLS] = turned[2, odd, :, 0 : CELLS - 256]
+                turned[c, pl.ds(r, 8, stride=ROWS), :] = value[:, 128 * c : 128 * (c + 1)]
+        ready[at, :, 0:128] = turned[0]
+        ready[at, :, 128:256] = turned[1]
+        ready[at, :, 256:CELLS] = turned[2, :, 0 : CELLS - 256]
+        leave(at).start()
+        return 0
+
+    lax.fori_loop(0, QUADS, one, 0)
+
+    def left(at, _):
+        leave(at).wait()
+        return 0
+
+    lax.fori_loop(0, QUADS, left, 0)
 
 
 def local(fields, inv_cos, coupling_lon, coupling_lat, polar_rows, bands):
+    stay = functools.partial(pltpu.with_memory_space_constraint, memory_space=pltpu.HBM)
     smem, vmem, anywhere = (pl.BlockSpec(memory_space=space) for space in (pltpu.SMEM, pltpu.VMEM, pl.ANY))
     dma = pltpu.SemaphoreType.DMA
     pair_hi, pair_lo, one_hi, one_lo, waves_pair, waves_one = tables()
@@ -516,8 +533,8 @@
     pred, back = pl.pallas_call(
         kernel,
         out_shape=(
-            jax.ShapeDtypeStruct((ROWS, QUADS, 8, WIDE), f32),
-            jax.ShapeDtypeStruct((UNITS, 8, WIDE), f32),
+            pltpu.VMEM((ROWS, QUADS, 8, WIDE), f32),
+            pltpu.VMEM((UNITS, 8, WIDE), f32),
         ),
         in_specs=[vmem] + [smem] * 5 + [anywhere] * 4 + [vmem] * 2,
         out_specs=(vmem, vmem),
@@ -542,34 +559,25 @@
             dma((3, PARTS)), dma((7, PARTS)), dma((3,)),
         ],
         compiler_params=pltpu.CompilerParams(
-            collective_id=0, has_side_effects=True, vmem_limit_bytes=60 * 2**20
+            collective_id=0, has_side_effects=True, vmem_limit_bytes=40 * 2**20
         ),
     )(
-        fields.reshape(F * LEV * ROWS, CELLS),
-        inv_cos,
-        coupling_lon,
-        coupling_lat,
-        polar_rows,
-        bands,
-        jnp.asarray(pair_hi), jnp.asarray(pair_lo), jnp.asarray(one_hi), jnp.asarray(one_lo),
-        jnp.asarray(waves_pair), jnp.asarray(waves_one),
+        stay(fields.reshape(F * LEV * ROWS, CELLS)),
+        *(stay(x) for x in (inv_cos, coupling_lon, coupling_lat, polar_rows, bands)),
+        *(stay(jnp.asarray(x)) for x in (pair_hi, pair_lo, one_hi, one_lo, waves_pair, waves_one)),
     )
     out = pl.pallas_call(
         place,
-        grid=(GROUPS, F // 2),
-        out_shape=jax.ShapeDtypeStruct((F, GROUPS, 8 * ROWS, CELLS), f32),
-        in_specs=[
-            smem,
-            pl.BlockSpec((ROWS, 1, 2, 8, WIDE), lambda g, pair: (0, g, pair, 0, 0)),
-            pl.BlockSpec((CAP, 1, 2, 8, WIDE), lambda g, pair: (0, g, pair, 0, 0)),
+        out_shape=jax.ShapeDtypeStruct((QUADS, 8 * ROWS, CELLS), f32),
+        in_specs=[smem, vmem, vmem],
+        out_specs=anywhere,
+        scratch_shapes=[
+            pltpu.VMEM((3, 8 * ROWS, 128), f32),
+            pltpu.VMEM((QUADS, 8 * ROWS, CELLS), f32),
+            dma((QUADS,)),
         ],
-        out_specs=pl.BlockSpec((2, 1, 8 * ROWS, CELLS), lambda g, pair: (pair, g, 0, 0)),
-        scratch_shapes=[pltpu.VMEM((3, 2, 8 * ROWS, 128), f32)],
-    )(
-        polar_rows,
-        pred.reshape(ROWS, GROUPS, F, 8, WIDE),
-        back.reshape(CAP, GROUPS, F, 8, WIDE),
-    )
+        compiler_params=pltpu.CompilerParams(vmem_limit_bytes=24 * 2**20),
+    )(stay(polar_rows), pred, back)
     return out.reshape(F, LEV, ROWS, CELLS)
 
 

time: 95.2 us -> 82.9 us (0.87)
  Pallas kernels: 93.9 us -> 81.8 us
    pallas_call x2, Pallas kernels: 93.9 us -> 81.8 us  [the longest x1 76.9 us: local(): pl.pallas_call(kernel, out_shape=(pltpu.VMEM((ROWS, QUADS, 8, WIDE), f32)...]
where the time goes in v3:
time: 82.9 us; the launch traced here: 81.8 us
  Pallas kernels  81.8 us (99%)
    pallas_call x1, Pallas kernels, local(): pl.pallas_call(kernel, out_shape=(pltpu.VMEM((ROWS, QUADS, 8, WIDE), f32)...  76.9 us
    pallas_call x1, Pallas kernels, local(): pl.pallas_call(place, out_shape=jax.ShapeDtypeStruct((QUADS, 8 * ROWS, CE...  4.94 us

profile of v3, /device:TPU:0, one launch (start us, length us, event | category | flops | bytes accessed | tf_op | source)
XLA Modules:
  0.0 81.8 jit_solution(11384616110130220411)
XLA Ops:
  0.0 76.9 %shard_map.118 = (f32[16,24,8,384]{3,2,1,0:T(8,128)S(1)}, f32[336,8,384]{2,1,0:T(8,128)S(1)}) custom-call(f32[3072,360]{1,0:T(8,128)} %bitcast.2, f32[16]{0:T(128)} %inv_cos.1, f32[6,6]{1,0:T(8,128)} %c_lon.1, f32[6,6]{1,0:T(8,128)} %c_lat.1, s32[56]{0:T(128)} %polar_rows.3, s32[56]{0:T(128)} %bands.1, bf16[3,768,512]{2,1,0:T(8,128)(2,1)} %constant.12.clone.pair_hi, ...), custom_call_target="tpu_custom_call" | custom-call | tf_op jit(solution)/shard_map/pallas_call | solution.py:533
  76.9 4.9 %shard_map.119 = f32[24,128,360]{2,1,0:T(8,128)} custom-call(s32[56]{0:T(128)} %polar_rows.3, f32[16,24,8,384]{3,2,1,0:T(8,128)S(1)} %get-tuple-element.7.pred, f32[336,8,384]{2,1,0:T(8,128)S(1)} %get-tuple-element.8.back), custom_call_target="tpu_custom_call" | custom-call | tf_op jit(solution)/shard_map/pallas_call | solution.py:569

commit v4 on v3

--- a/solution.py
+++ b/solution.py
@@ -16,11 +16,13 @@
 GROUPS, QUADS = LEV // 8, LEV // 8 * F
 SLOT = QUADS
 UNITS = CAP * SLOT
-BLOCK = 6
+BLOCK = 3
 SEGMENT = PARTS * BLOCK
-HELP_SEGMENTS = ((0, 3), (1, 4))
-OWN_SEGMENTS = (2, 5, 6)
-BATCH = 8 * BLOCK
+HELP_SEGMENTS = ((0, 3, 6, 9, 12), (1, 4, 7, 10))
+OWN_SEGMENTS = (2, 5, 8, 11, 13)
+MOST = 5
+ROOM = 4
+BATCH = 8 * ROOM
 HALF = 1.0 / math.sqrt(2.0)
 
 
@@ -52,22 +54,25 @@
         single[at, :CELLS, :128] = np.cos(angles(waves))
         single[at, :CELLS, 128:] = -np.sin(angles(waves))
         waves_single[at, 0] = np.concatenate([waves] * 2)
-    return (*halves(pair), *halves(single), waves_pair, waves_single)
+    gaps = np.zeros((WIDE, WIDE))
+    for d, factor in ((1, 45.0), (2, -9.0), (3, 1.0)):
+        gaps += factor * (np.roll(np.eye(WIDE), d, axis=0) - np.roll(np.eye(WIDE), -d, axis=0))
+    return (*halves(pair), *halves(single), waves_pair, waves_single, gaps.astype(ml_dtypes.bfloat16))
 
 
 def kernel(
-    fields, inv_cos, c_lon, c_lat, polar_rows, bands, pair_hi, pair_lo, one_hi, one_lo, waves_pair, waves_one,
+    fields, inv_cos, c_lon, c_lat, polar_rows, bands, pair_hi, pair_lo, one_hi, one_lo, waves_pair, waves_one, gap_table,
     pred, back,
-    grid, lon_out, lon_in, slots, relay, pieces, result, spec, t_ph, t_pl, t_oh, t_ol, turned,
-    tab_sem, lon_ss, lon_rs, lat_ss, lat_rs, help_ss, help_rs, own_ss, own_rs, self_sem, ret_ss, ret_rs, ret_self,
+    grid, lon_out, lon_in, slots, relay, pieces, result, spec, t_ph, t_pl, t_oh, t_ol, turned, row, along,
+    tab_sem, lon_ss, lon_rs, lat_ss, lat_rs, slot_ss, help_rs, own_rs, ret_ss, ret_rs,
 ):
     t, i = lax.axis_index("lat"), lax.axis_index("lon")
     north, south = t < 2, t >= 14
     polar = north | south
-    up = (t >= 2) & (t < 6)
-    down = (t >= 10) & (t < 14)
+    up = ((t >= 2) & (t < 4)) | ((t >= 12) & (t < 14))
+    down = ((t >= 4) & (t < 6)) | ((t >= 10) & (t < 12))
     helper = up | down
-    host = jnp.where(polar, t, jnp.where(up, lax.rem(t + 12, 16), lax.rem(t + 4, 16)))
+    host = jnp.where(polar, t, lax.rem(t + jnp.where(t < 6, 12, 4), 16))
     flip = host >= 14
     first = jnp.where(host < 2, host, jnp.where(flip, host - 12, 0)) * CAP
 
@@ -201,94 +206,100 @@
         others(act)
         act(i)
 
+    def await_bytes(ref, sem):
+        pltpu.make_async_copy(ref, ref, sem).wait()
+
     def units(segment, j):
         return pl.ds(segment * SEGMENT + j * BLOCK, BLOCK)
 
     def own_segment(block):
-        return jnp.where(block == 0, OWN_SEGMENTS[0], OWN_SEGMENTS[1] - 1 + block)
+        return 2 + 3 * block - block // 4
 
     def help_send(which, block, j):
         return pltpu.make_async_remote_copy(
-            src_ref=slots.at[units(HELP_SEGMENTS[which][block], j)], dst_ref=relay.at[block, j],
-            send_sem=help_ss.at[which, block, j], recv_sem=help_rs.at[block, j],
-            device_id=(lax.rem(t + (4, 12)[which], 16), i), device_id_type=MESH,
+            src_ref=slots.at[units(3 * block + which, j)], dst_ref=relay.at[block, j],
+            send_sem=slot_ss, recv_sem=help_rs.at[block],
+            device_id=(lax.rem(t + jnp.where(flip, (4, 12)[which], (12, 4)[which]), 16), i), device_id_type=MESH,
         )
 
     def own_send(block, p, j):
         return pltpu.make_async_remote_copy(
             src_ref=slots.at[units(own_segment(block), j)], dst_ref=pieces.at[block, p],
-            send_sem=own_ss.at[block, j], recv_sem=own_rs.at[block, p],
+            send_sem=slot_ss, recv_sem=own_rs.at[block],
             device_id=(t, j), device_id_type=MESH,
         )
 
     def own_local(block):
         return pltpu.make_async_copy(
-            slots.at[units(own_segment(block), i)], pieces.at[block, i], self_sem.at[block]
+            slots.at[units(own_segment(block), i)], pieces.at[block, i], own_rs.at[block]
         )
 
     def relay_send(block, p, j):
         return pltpu.make_async_remote_copy(
             src_ref=relay.at[block, j], dst_ref=pieces.at[block, p],
-            send_sem=own_ss.at[block, j], recv_sem=own_rs.at[block, p],
+            send_sem=slot_ss, recv_sem=own_rs.at[block],
             device_id=(t, j), device_id_type=MESH,
         )
 
     def relay_local(block):
-        return pltpu.make_async_copy(relay.at[block, i], pieces.at[block, i], self_sem.at[block])
+        return pltpu.make_async_copy(relay.at[block, i], pieces.at[block, i], own_rs.at[block])
 
     def step(at, _):
-        n, g = at // GROUPS, lax.rem(at, GROUPS)
-        n = jnp.where(n < ROWS, n, jnp.where(n < ROWS + 3, n - ROWS, n - 6))
+        n = jnp.where(at < ROWS, at, jnp.where(at < ROWS + 3, at - ROWS, at - 6))
         r = jnp.where(flip, ROWS - 1 - n, n)
         scale = inv_cos[r] * (1.0 / 60.0)
-        centre, along_lon, along_lat = [], [], []
-        for f in range(F):
-            k = (f % 2) * 16 + r
-            east = pltpu.roll(lon_in[0, g, f // 2], lax.rem(104 + 128 - 4 * k, 128), axis=1)
-            west = pltpu.roll(lon_in[1, g, f // 2], lax.rem(125 + 128 - 4 * k, 128), axis=1)
-            mid = grid[r + 3, g, f]
-            halo = jnp.where((lane >= 104) & (lane < 107), east, jnp.where(lane >= 125, west, 0.0))
-            cells = jnp.concatenate([mid[:, :256], mid[:, 256:] + halo], axis=1)
-            centre.append(mid)
-
-            def at_cell(d):
-                return pltpu.roll(cells, (WIDE - d) % WIDE, axis=1)
-
-            along_lon.append(
-                (45.0 * (at_cell(1) - at_cell(-1)) - 9.0 * (at_cell(2) - at_cell(-2)) + (at_cell(3) - at_cell(-3)))
-                * scale
-            )
-
-            def at_row(d):
-                return grid[r + 3 + d, g, f]
-
-            along_lat.append(
-                (45.0 * (at_row(1) - at_row(-1)) - 9.0 * (at_row(2) - at_row(-2)) + (at_row(3) - at_row(-3)))
-                * (1.0 / 60.0)
-            )
-        for f in range(F):
-            total = centre[f]
-            for h in range(F):
-                total = total + c_lon[f, h] * along_lon[h] + c_lat[f, h] * along_lat[h]
-            pred[r, g * F + f] = jnp.where(lax.broadcasted_iota(jnp.int32, (8, WIDE), 1) < CELLS, total, 0.0)
-
-        @pl.when(polar & (g == GROUPS - 1) & (n >= 2))
+        for g in range(GROUPS):
+            for f in range(F):
+                k = (f % 2) * 16 + r
+                east = pltpu.roll(lon_in[0, g, f // 2], lax.rem(104 + 128 - 4 * k, 128), axis=1)
+                west = pltpu.roll(lon_in[1, g, f // 2], lax.rem(125 + 128 - 4 * k, 128), axis=1)
+                halo = jnp.where((lane >= 104) & (lane < 107), east, jnp.where(lane >= 125, west, 0.0))
+                here = slice((g * F + f) * 8, (g * F + f + 1) * 8)
+                row[here, 0:256] = grid[r + 3, g, f, :, 0:256]
+                row[here, 256:WIDE] = grid[r + 3, g, f, :, 256:WIDE] + halo
+        top = row[...].astype(jnp.bfloat16)
+        low = (row[...] - top.astype(jnp.float32)).astype(jnp.bfloat16)
+        both = jnp.dot(
+            jnp.concatenate([top, low], axis=0), gap_table[...], preferred_element_type=jnp.float32
+        )
+        along[...] = (both[: QUADS * 8] + both[QUADS * 8 :]) * scale
+
+        for g in range(GROUPS):
+            along_lat, along_lon = [], []
+            for f in range(F):
+
+                def at_row(d):
+                    return grid[r + 3 + d, g, f]
+
+                along_lat.append(
+                    (45.0 * (at_row(1) - at_row(-1)) - 9.0 * (at_row(2) - at_row(-2)) + (at_row(3) - at_row(-3)))
+                    * (1.0 / 60.0)
+                )
+                along_lon.append(along[(g * F + f) * 8 : (g * F + f + 1) * 8, :])
+            for f in range(F):
+                total = grid[r + 3, g, f]
+                for h in range(F):
+                    total = total + c_lon[f, h] * along_lon[h] + c_lat[f, h] * along_lat[h]
+                pred[r, g * F + f, :, 0:256] = total[:, 0:256]
+                pred[r, g * F + f, :, 256:WIDE] = jnp.where(lane < CELLS - 256, total[:, 256:], 0.0)
+
+        @pl.when(polar & (n >= 2))
         def _():
             s = jnp.where(flip, CAP - 1 - (n - 2), n - 2)
-            row = jnp.clip(polar_rows[first + s] - t * ROWS, 0, ROWS - 1)
+            chosen = jnp.clip(polar_rows[first + s] - t * ROWS, 0, ROWS - 1)
             for q in range(SLOT):
-                slots[(n - 2) * SLOT + q] = pred[row, q]
+                slots[(n - 2) * SLOT + q] = pred[chosen, q]
 
             for which in range(2):
-                for block in range(2):
-
-                    @pl.when(n == 2 * HELP_SEGMENTS[which][block] + 3)
+                for block, segment in enumerate(HELP_SEGMENTS[which]):
+
+                    @pl.when(n == segment + 2)
                     def _():
                         everyone(lambda j: help_send(which, block, j).start())
 
             for block, segment in enumerate(OWN_SEGMENTS):
 
-                @pl.when(n == 2 * segment + 3)
+                @pl.when(n == segment + 2)
                 def _():
                     others(lambda j: own_send(block, i, j).start())
                     own_local(block).start()
@@ -296,7 +307,7 @@
         return 0
 
     def rows_from(lo, hi):
-        lax.fori_loop(lo * GROUPS, hi * GROUPS, step, 0)
+        lax.fori_loop(lo, hi, step, 0)
 
     @pl.when(polar & jnp.logical_not(flip))
     def _():
@@ -311,19 +322,19 @@
     def ret_own(block, p, j):
         return pltpu.make_async_remote_copy(
             src_ref=result.at[block, p], dst_ref=back.at[units(own_segment(block), j)],
-            send_sem=ret_ss.at[block, p], recv_sem=ret_rs.at[block, j],
+            send_sem=ret_ss, recv_sem=ret_rs,
             device_id=(t, p), device_id_type=MESH,
         )
 
     def ret_own_local(block):
         return pltpu.make_async_copy(
-            result.at[block, i], back.at[units(own_segment(block), i)], ret_self.at[block]
+            result.at[block, i], back.at[units(own_segment(block), i)], ret_rs
         )
 
     def ret_help(which, block, p, j):
         return pltpu.make_async_remote_copy(
             src_ref=result.at[block, p], dst_ref=back.at[units(3 * block + which, j)],
-            send_sem=ret_ss.at[block, p], recv_sem=ret_rs.at[3 + 2 * which + block, j],
+            send_sem=ret_ss, recv_sem=ret_rs,
             device_id=(host, p), device_id_type=MESH,
         )
 
@@ -337,27 +348,12 @@
         cross = lax.dot_general(top, tail, dims, preferred_element_type=jnp.float32)
         return both[:BATCH] + (both[BATCH:] + cross)
 
-    def band_column(block):
-        segment = jnp.where(polar, own_segment(block), 3 * block + jnp.where(up, 0, 1))
-        start = segment * SEGMENT + i * BLOCK
-        unit_of = lax.broadcasted_iota(jnp.int32, (BATCH, 1), 0) // 8
-        column = jnp.zeros((BATCH, 1), jnp.int32)
-        for n in range(BLOCK):
-            s = jnp.minimum((start + n) // SLOT, CAP - 1)
-            s = jnp.where(flip, CAP - 1 - s, s)
-            column = jnp.where(unit_of == n, bands[first + s], column)
-        return column
+    def band_of(block):
+        s = jnp.where(polar, own_segment(block), 3 * block + jnp.where(up, 0, 1))
+        return bands[first + jnp.where(flip, CAP - 1 - s, s)]
 
     def filter_block(block, _):
-        @pl.when(polar)
-        def _():
-            others(lambda p: own_send(block, p, i).wait_recv())
-            own_local(block).wait()
-
-        @pl.when(helper)
-        def _():
-            others(lambda p: relay_send(block, p, i).wait_recv())
-            relay_local(block).wait()
+        await_bytes(pieces.at[block], own_rs.at[block])
 
         def forward(n, _):
             x = [pieces[block, p, n] for p in range(PARTS)]
@@ -376,17 +372,17 @@
             return 0
 
         lax.fori_loop(0, BLOCK, forward, 0)
-        column = band_column(block)
+        band = band_of(block)
         for m in range(3):
             here = slice(m * 2 * WIDE, (m + 1) * 2 * WIDE)
             waves = matmul(spec[:, here], t_ph[m], t_pl[m], False)
-            waves = jnp.where(waves_pair[m] < column, waves * (2.0 / LENGTH), 0.0)
+            waves = jnp.where(waves_pair[m] < band, waves * (2.0 / LENGTH), 0.0)
             spec[:, here] = matmul(waves, t_ph[m], t_pl[m], True)
         for m in range(2):
             here = slice((6 + m) * WIDE, (7 + m) * WIDE)
             waves = matmul(spec[:, here], t_oh[m], t_ol[m], False)
             factor = jnp.where(waves_one[m] == 0, 1.0 / LENGTH, 2.0 / LENGTH)
-            waves = jnp.where(waves_one[m] < column, waves * factor, 0.0)
+            waves = jnp.where(waves_one[m] < band, waves * factor, 0.0)
             spec[:, here] = matmul(waves, t_oh[m], t_ol[m], True)
 
         def inverse(n, _):
@@ -421,22 +417,26 @@
         return 0
 
     def pass_on(block):
-        @pl.when(helper)
-        def _():
-            def one(j):
-                help_send(0, block, j).wait_recv()
-                relay_send(block, i, j).start()
-
-            others(one)
-            help_send(0, block, i).wait_recv()
-            relay_local(block).start()
+        await_bytes(relay.at[block], help_rs.at[block])
+        others(lambda j: relay_send(block, i, j).start())
+        relay_local(block).start()
 
     for load in loads:
         load.wait()
-    pass_on(0)
-    busy = jnp.where(polar | helper, 1, 0)
-    lax.fori_loop(0, busy, filter_block, 0)
-    pass_on(1)
+    blocks = jnp.where(polar | up, MOST, jnp.where(down, len(HELP_SEGMENTS[1]), 0))
+
+    def helped(block, _):
+        pass_on(block)
+
+        @pl.when(block > 0)
+        def _():
+            filter_block(block - 1, 0)
+
+        return 0
+
+    lax.fori_loop(0, jnp.where(helper, blocks, 0), helped, 0)
+    ready = jnp.where(helper, blocks - 1, 0)
+    lax.fori_loop(ready, jnp.where(helper, blocks, jnp.where(polar, 2, 0)), filter_block, 0)
 
     @pl.when(polar & jnp.logical_not(flip))
     def _():
@@ -452,7 +452,7 @@
         wait_below()
 
     rows_from(ROWS + jnp.where(polar, 3, 0), ROWS + 6)
-    lax.fori_loop(1, jnp.where(polar, 3, jnp.where(helper, 2, 1)), filter_block, 0)
+    lax.fori_loop(2, jnp.where(polar, blocks, 2), filter_block, 0)
 
     for copy in lon_copies:
         copy.wait_send()
@@ -465,23 +465,23 @@
     def _():
         north_copy.wait_send()
 
-    @pl.when(helper)
-    def _():
-        for block in range(2):
-            others(lambda j: relay_send(block, i, j).wait_send())
-            everyone(lambda p: ret_help(0, block, p, i).wait_send())
+    few = len(HELP_SEGMENTS[1])
+
+    @pl.when(up)
+    def _():
+        await_bytes(relay.at[:, pl.ds(0, PARTS - 1)], slot_ss)
+        await_bytes(result, ret_ss)
+
+    @pl.when(down)
+    def _():
+        await_bytes(relay.at[pl.ds(0, few), pl.ds(0, PARTS - 1)], slot_ss)
+        await_bytes(result.at[pl.ds(0, few)], ret_ss)
 
     @pl.when(polar)
     def _():
-        for block in range(3):
-            others(lambda j: own_send(block, i, j).wait_send())
-            others(lambda p: ret_own(block, p, i).wait_send())
-            others(lambda j: ret_own(block, i, j).wait_recv())
-            ret_own_local(block).wait()
-        for which in range(2):
-            for block in range(2):
-                everyone(lambda j: help_send(which, block, j).wait_send())
-                everyone(lambda j: ret_help(which, block, i, j).wait_recv())
+        await_bytes(slots.at[pl.ds(0, UNITS - MOST * BLOCK)], slot_ss)
+        await_bytes(result.at[:, pl.ds(0, PARTS - 1)], ret_ss)
+        await_bytes(back, ret_rs)
 
 
 def place(polar_rows, pred, back, out, turned, ready, sems):
@@ -528,7 +528,7 @@
     stay = functools.partial(pltpu.with_memory_space_constraint, memory_space=pltpu.HBM)
     smem, vmem, anywhere = (pl.BlockSpec(memory_space=space) for space in (pltpu.SMEM, pltpu.VMEM, pl.ANY))
     dma = pltpu.SemaphoreType.DMA
-    pair_hi, pair_lo, one_hi, one_lo, waves_pair, waves_one = tables()
+    constants = tables()
     f32, bf16 = jnp.float32, jnp.bfloat16
     pred, back = pl.pallas_call(
         kernel,
@@ -536,27 +536,27 @@
             pltpu.VMEM((ROWS, QUADS, 8, WIDE), f32),
             pltpu.VMEM((UNITS, 8, WIDE), f32),
         ),
-        in_specs=[vmem] + [smem] * 5 + [anywhere] * 4 + [vmem] * 2,
+        in_specs=[vmem] + [smem] * 5 + [anywhere] * 4 + [vmem] * 3,
         out_specs=(vmem, vmem),
         scratch_shapes=[
             pltpu.VMEM((ROWS + 6, GROUPS, F, 8, WIDE), f32),
             pltpu.VMEM((2, GROUPS, F // 2, 8, 128), f32),
             pltpu.VMEM((2, GROUPS, F // 2, 8, 128), f32),
             pltpu.VMEM((UNITS, 8, WIDE), f32),
-            pltpu.VMEM((2, PARTS, BLOCK, 8, WIDE), f32),
-            pltpu.VMEM((3, PARTS, BLOCK, 8, WIDE), f32),
-            pltpu.VMEM((3, PARTS, BLOCK, 8, WIDE), f32),
+            pltpu.VMEM((MOST, PARTS, BLOCK, 8, WIDE), f32),
+            pltpu.VMEM((MOST, PARTS, BLOCK, 8, WIDE), f32),
+            pltpu.VMEM((MOST, PARTS, BLOCK, 8, WIDE), f32),
             pltpu.VMEM((BATCH, 8 * WIDE), f32),
             pltpu.VMEM((3, 2 * WIDE, 512), bf16),
             pltpu.VMEM((3, 2 * WIDE, 512), bf16),
             pltpu.VMEM((2, WIDE, 256), bf16),
             pltpu.VMEM((2, WIDE, 256), bf16),
             pltpu.VMEM((3, 2, 128, 128), f32),
+            pltpu.VMEM((QUADS * 8, WIDE), f32),
+            pltpu.VMEM((QUADS * 8, WIDE), f32),
             dma((4,)),
             dma((2,)), dma((2,)), dma((2,)), dma((2,)),
-            dma((2, 2, PARTS)), dma((2, PARTS)),
-            dma((3, PARTS)), dma((3, PARTS)), dma((3,)),
-            dma((3, PARTS)), dma((7, PARTS)), dma((3,)),
+            dma, dma((MOST,)), dma((MOST,)), dma, dma,
         ],
         compiler_params=pltpu.CompilerParams(
             collective_id=0, has_side_effects=True, vmem_limit_bytes=40 * 2**20
@@ -564,7 +564,7 @@
     )(
         stay(fields.reshape(F * LEV * ROWS, CELLS)),
         *(stay(x) for x in (inv_cos, coupling_lon, coupling_lat, polar_rows, bands)),
-        *(stay(jnp.asarray(x)) for x in (pair_hi, pair_lo, one_hi, one_lo, waves_pair, waves_one)),
+        *(stay(jnp.asarray(x)) for x in constants),
     )
     out = pl.pallas_call(
         place,

time: 82.9 us -> 78.5 us (0.947); the launches traced: 81.8 us -> 78.4 us
  Pallas kernels: 81.8 us -> 78.4 us
    pallas_call x1, Pallas kernels: 76.9 us -> 73.4 us  [local(): pl.pallas_call(kernel, out_shape=(pltpu.VMEM((ROWS, QUADS, 8, WIDE), f32)...]
where the time goes in v4:
time: 78.5 us; the launch traced here: 78.4 us
  Pallas kernels  78.4 us (100%)
    pallas_call x1, Pallas kernels, local(): pl.pallas_call(kernel, out_shape=(pltpu.VMEM((ROWS, QUADS, 8, WIDE), f32)...  73.4 us
    pallas_call x1, Pallas kernels, local(): pl.pallas_call(place, out_shape=jax.ShapeDtypeStruct((QUADS, 8 * ROWS, CE...  4.94 us

profile of v4, /device:TPU:0, one launch (start us, length us, event | category | flops | bytes accessed | tf_op | source)
XLA Modules:
  0.0 78.4 jit_solution(13606318811269487462)
XLA Ops:
  0.0 73.4 %shard_map.127 = (f32[16,24,8,384]{3,2,1,0:T(8,128)S(1)}, f32[336,8,384]{2,1,0:T(8,128)S(1)}) custom-call(f32[3072,360]{1,0:T(8,128)} %bitcast.2, f32[16]{0:T(128)} %inv_cos.1, f32[6,6]{1,0:T(8,128)} %c_lon.1, f32[6,6]{1,0:T(8,128)} %c_lat.1, s32[56]{0:T(128)} %polar_rows.3, s32[56]{0:T(128)} %bands.1, bf16[3,768,512]{2,1,0:T(8,128)(2,1)} %constant.14.clone.pair_hi, ...), custom_call_target="tpu_custom_call" | custom-call | tf_op jit(solution)/shard_map/pallas_call | solution.py:533
  73.4 4.9 %shard_map.128 = f32[24,128,360]{2,1,0:T(8,128)} custom-call(s32[56]{0:T(128)} %polar_rows.3, f32[16,24,8,384]{3,2,1,0:T(8,128)S(1)} %get-tuple-element.7.pred, f32[336,8,384]{2,1,0:T(8,128)S(1)} %get-tuple-element.8.back), custom_call_target="tpu_custom_call" | custom-call | tf_op jit(solution)/shard_map/pallas_call | solution.py:569

commit v5 on v4

--- a/solution.py
+++ b/solution.py
@@ -18,9 +18,10 @@
 UNITS = CAP * SLOT
 BLOCK = 3
 SEGMENT = PARTS * BLOCK
-HELP_SEGMENTS = ((0, 3, 6, 9, 12), (1, 4, 7, 10))
-OWN_SEGMENTS = (2, 5, 8, 11, 13)
-MOST = 5
+HELP_SEGMENTS = ((0, 3, 6, 9), (1, 4, 7, 10))
+OWN_SEGMENTS = (2, 5, 8, 11, 12, 13)
+OWN, MANY, FEW = (len(entries) for entries in (OWN_SEGMENTS, *HELP_SEGMENTS))
+MOST = max(OWN, MANY, FEW)
 ROOM = 4
 BATCH = 8 * ROOM
 HALF = 1.0 / math.sqrt(2.0)
@@ -206,6 +207,12 @@
         others(act)
         act(i)
 
+    def pick(entries, block):
+        chosen = entries[0]
+        for n, entry in enumerate(entries):
+            chosen = jnp.where(block == n, entry, chosen)
+        return chosen
+
     def await_bytes(ref, sem):
         pltpu.make_async_copy(ref, ref, sem).wait()
 
@@ -213,11 +220,14 @@
         return pl.ds(segment * SEGMENT + j * BLOCK, BLOCK)
 
     def own_segment(block):
-        return 2 + 3 * block - block // 4
+        return pick(OWN_SEGMENTS, block)
+
+    def help_segment(which, block):
+        return pick(HELP_SEGMENTS[which], block)
 
     def help_send(which, block, j):
         return pltpu.make_async_remote_copy(
-            src_ref=slots.at[units(3 * block + which, j)], dst_ref=relay.at[block, j],
+            src_ref=slots.at[units(help_segment(which, block), j)], dst_ref=relay.at[block, j],
             send_sem=slot_ss, recv_sem=help_rs.at[block],
             device_id=(lax.rem(t + jnp.where(flip, (4, 12)[which], (12, 4)[which]), 16), i), device_id_type=MESH,
         )
@@ -333,7 +343,7 @@
 
     def ret_help(which, block, p, j):
         return pltpu.make_async_remote_copy(
-            src_ref=result.at[block, p], dst_ref=back.at[units(3 * block + which, j)],
+            src_ref=result.at[block, p], dst_ref=back.at[units(help_segment(which, block), j)],
             send_sem=ret_ss, recv_sem=ret_rs,
             device_id=(host, p), device_id_type=MESH,
         )
@@ -349,7 +359,7 @@
         return both[:BATCH] + (both[BATCH:] + cross)
 
     def band_of(block):
-        s = jnp.where(polar, own_segment(block), 3 * block + jnp.where(up, 0, 1))
+        s = jnp.where(polar, own_segment(block), jnp.where(up, help_segment(0, block), help_segment(1, block)))
         return bands[first + jnp.where(flip, CAP - 1 - s, s)]
 
     def filter_block(block, _):
@@ -423,7 +433,7 @@
 
     for load in loads:
         load.wait()
-    blocks = jnp.where(polar | up, MOST, jnp.where(down, len(HELP_SEGMENTS[1]), 0))
+    blocks = jnp.where(polar, OWN, jnp.where(up, MANY, jnp.where(down, FEW, 0)))
 
     def helped(block, _):
         pass_on(block)
@@ -465,22 +475,20 @@
     def _():
         north_copy.wait_send()
 
-    few = len(HELP_SEGMENTS[1])
-
     @pl.when(up)
     def _():
-        await_bytes(relay.at[:, pl.ds(0, PARTS - 1)], slot_ss)
-        await_bytes(result, ret_ss)
+        await_bytes(relay.at[pl.ds(0, MANY), pl.ds(0, PARTS - 1)], slot_ss)
+        await_bytes(result.at[pl.ds(0, MANY)], ret_ss)
 
     @pl.when(down)
     def _():
-        await_bytes(relay.at[pl.ds(0, few), pl.ds(0, PARTS - 1)], slot_ss)
-        await_bytes(result.at[pl.ds(0, few)], ret_ss)
+        await_bytes(relay.at[pl.ds(0, FEW), pl.ds(0, PARTS - 1)], slot_ss)
+        await_bytes(result.at[pl.ds(0, FEW)], ret_ss)
 
     @pl.when(polar)
     def _():
-        await_bytes(slots.at[pl.ds(0, UNITS - MOST * BLOCK)], slot_ss)
-        await_bytes(result.at[:, pl.ds(0, PARTS - 1)], ret_ss)
+        await_bytes(slots.at[pl.ds(0, UNITS - OWN * BLOCK)], slot_ss)
+        await_bytes(result.at[pl.ds(0, OWN), pl.ds(0, PARTS - 1)], ret_ss)
         await_bytes(back, ret_rs)
 
 

time: 78.5 us -> 73.6 us (0.938)
  Pallas kernels: 78.4 us -> 72.9 us
    pallas_call x1, Pallas kernels: 73.4 us -> 68 us  [local(): pl.pallas_call(kernel, out_shape=(pltpu.VMEM((ROWS, QUADS, 8, WIDE), f32)...]
where the time goes in v5:
time: 73.6 us; the launch traced here: 72.9 us
  Pallas kernels  72.9 us (99%)
    pallas_call x1, Pallas kernels, local(): pl.pallas_call(kernel, out_shape=(pltpu.VMEM((ROWS, QUADS, 8, WIDE), f32)...  68 us
    pallas_call x1, Pallas kernels, local(): pl.pallas_call(place, out_shape=jax.ShapeDtypeStruct((QUADS, 8 * ROWS, CE...  4.94 us

profile of v5, /device:TPU:0, one launch (start us, length us, event | category | flops | bytes accessed | tf_op | source)
XLA Modules:
  0.0 72.9 jit_solution(16522722536810072966)
XLA Ops:
  0.0 68.0 %shard_map.127 = (f32[16,24,8,384]{3,2,1,0:T(8,128)S(1)}, f32[336,8,384]{2,1,0:T(8,128)S(1)}) custom-call(f32[3072,360]{1,0:T(8,128)} %bitcast.2, f32[16]{0:T(128)} %inv_cos.1, f32[6,6]{1,0:T(8,128)} %c_lon.1, f32[6,6]{1,0:T(8,128)} %c_lat.1, s32[56]{0:T(128)} %polar_rows.3, s32[56]{0:T(128)} %bands.1, bf16[3,768,512]{2,1,0:T(8,128)(2,1)} %constant.14.clone.pair_hi, ...), custom_call_target="tpu_custom_call" | custom-call | tf_op jit(solution)/shard_map/pallas_call | solution.py:541
  68.0 4.9 %shard_map.128 = f32[24,128,360]{2,1,0:T(8,128)} custom-call(s32[56]{0:T(128)} %polar_rows.3, f32[16,24,8,384]{3,2,1,0:T(8,128)S(1)} %get-tuple-element.7.pred, f32[336,8,384]{2,1,0:T(8,128)S(1)} %get-tuple-element.8.back), custom_call_target="tpu_custom_call" | custom-call | tf_op jit(solution)/shard_map/pallas_call | solution.py:577

commit v6 on v5

--- a/solution.py
+++ b/solution.py
@@ -62,9 +62,9 @@
 
 
 def kernel(
-    fields, inv_cos, c_lon, c_lat, polar_rows, bands, pair_hi, pair_lo, one_hi, one_lo, waves_pair, waves_one, gap_table,
+    arriving, inv_cos, c_lon, c_lat, polar_rows, bands, pair_hi, pair_lo, one_hi, one_lo, waves_pair, waves_one, gap_table,
     pred, back,
-    grid, lon_out, lon_in, slots, relay, pieces, result, spec, t_ph, t_pl, t_oh, t_ol, turned, row, along,
+    grid, lon_out, lon_in, slots, relay, pieces, result, spec, t_ph, t_pl, t_oh, t_ol, turned, row, along, fields, in_sem,
     tab_sem, lon_ss, lon_rs, lat_ss, lat_rs, slot_ss, help_rs, own_rs, ret_ss, ret_rs,
 ):
     t, i = lax.axis_index("lat"), lax.axis_index("lon")
@@ -81,6 +81,13 @@
         pltpu.make_async_copy(src, dst, tab_sem.at[n])
         for n, (src, dst) in enumerate(((pair_hi, t_ph), (pair_lo, t_pl), (one_hi, t_oh), (one_lo, t_ol)))
     ]
+    def enter(at):
+        rows = pl.ds(pl.multiple_of(at * 128, 128), 128)
+        return pltpu.make_async_copy(arriving.at[rows], fields.at[rows], in_sem.at[at])
+
+    for g in range(GROUPS):
+        for f in range(F):
+            enter(f * GROUPS + g).start()
     for load in loads:
         load.start()
 
@@ -119,6 +126,7 @@
         for odd in range(2):
             f = 2 * pair + odd
             base = pl.multiple_of(f * LEV * ROWS + g * 128, 128)
+            enter(f * GROUPS + g).wait()
             turned[0, odd] = fields[pl.ds(base, 128), 0:128]
             turned[1, odd] = fields[pl.ds(base, 128), 128:256]
             turned[2, odd, :, 0 : CELLS - 256] = fields[pl.ds(base, 128), 256:CELLS]
@@ -544,7 +552,7 @@
             pltpu.VMEM((ROWS, QUADS, 8, WIDE), f32),
             pltpu.VMEM((UNITS, 8, WIDE), f32),
         ),
-        in_specs=[vmem] + [smem] * 5 + [anywhere] * 4 + [vmem] * 3,
+        in_specs=[anywhere] + [smem] * 5 + [anywhere] * 4 + [vmem] * 3,
         out_specs=(vmem, vmem),
         scratch_shapes=[
             pltpu.VMEM((ROWS + 6, GROUPS, F, 8, WIDE), f32),
@@ -562,6 +570,8 @@
             pltpu.VMEM((3, 2, 128, 128), f32),
             pltpu.VMEM((QUADS * 8, WIDE), f32),
             pltpu.VMEM((QUADS * 8, WIDE), f32),
+            pltpu.VMEM((F * LEV * ROWS, CELLS), f32),
+            dma((QUADS,)),
             dma((4,)),
             dma((2,)), dma((2,)), dma((2,)), dma((2,)),
             dma, dma((MOST,)), dma((MOST,)), dma, dma,

time: 73.6 us -> 72.4 us (0.984)
  Pallas kernels: 72.9 us -> 71.6 us
    pallas_call x1, Pallas kernels: 68 us -> 66.7 us  [local(): pl.pallas_call(kernel, out_shape=(pltpu.VMEM((ROWS, QUADS, 8, WIDE), f32)...]
where the time goes in v6:
time: 72.4 us; the launch traced here: 71.6 us
  Pallas kernels  71.6 us (99%)
    pallas_call x1, Pallas kernels, local(): pl.pallas_call(kernel, out_shape=(pltpu.VMEM((ROWS, QUADS, 8, WIDE), f32)...  66.7 us
    pallas_call x1, Pallas kernels, local(): pl.pallas_call(place, out_shape=jax.ShapeDtypeStruct((QUADS, 8 * ROWS, CE...  4.94 us

profile of v6, /device:TPU:0, one launch (start us, length us, event | category | flops | bytes accessed | tf_op | source)
XLA Modules:
  0.0 71.6 jit_solution(4449496182287607974)
XLA Ops:
  0.0 66.7 %shard_map.127 = (f32[16,24,8,384]{3,2,1,0:T(8,128)S(1)}, f32[336,8,384]{2,1,0:T(8,128)S(1)}) custom-call(f32[3072,360]{1,0:T(8,128)} %bitcast.2, f32[16]{0:T(128)} %inv_cos.1, f32[6,6]{1,0:T(8,128)} %c_lon.1, f32[6,6]{1,0:T(8,128)} %c_lat.1, s32[56]{0:T(128)} %polar_rows.3, s32[56]{0:T(128)} %bands.1, bf16[3,768,512]{2,1,0:T(8,128)(2,1)} %constant.14.clone.pair_hi, ...), custom_call_target="tpu_custom_call" | custom-call | tf_op jit(solution)/shard_map/pallas_call | solution.py:549
  66.7 4.9 %shard_map.128 = f32[24,128,360]{2,1,0:T(8,128)} custom-call(s32[56]{0:T(128)} %polar_rows.3, f32[16,24,8,384]{3,2,1,0:T(8,128)S(1)} %get-tuple-element.7.pred, f32[336,8,384]{2,1,0:T(8,128)S(1)} %get-tuple-element.8.back), custom_call_target="tpu_custom_call" | custom-call | tf_op jit(solution)/shard_map/pallas_call | solution.py:587
